TPU v7x, 32 devices: a whole 2x2x4 slice. The times are simulated.
32 devices in a mesh: dp: 8 (over z, y), tensor: 4 (over x, core).
Axes of the slice: x: 2, y: 2, z: 4, core: 2. Of those that a mesh axis runs over, the one named last changes fastest.
Arguments:
- tokens: bfloat16 [8192, 2048], P('dp'), may hold values from -6 to 6
- attention_gain: float32 [2048], replicated, may hold values from 0.5 to 1.5
- query_weight: bfloat16 [2048, 2048], P(None, 'tensor'), may hold values from -0.125 to 0.125
- key_weight: bfloat16 [2048, 1024], P(None, 'tensor'), may hold values from -0.125 to 0.125
- value_weight: bfloat16 [2048, 1024], P(None, 'tensor'), may hold values from -0.125 to 0.125
- query_gain: float32 [128], replicated, may hold values from 0.25 to 1.75
- key_gain: float32 [128], replicated, may hold values from 0.25 to 1.75
- output_weight: bfloat16 [2048, 2048], P('tensor'), may hold values from -1 to 1
- feedforward_gain: float32 [2048], replicated, may hold values from 0.5 to 1.5
- gate_weight: bfloat16 [2048, 6144], P(None, 'tensor'), may hold values from -0.125 to 0.125
- up_weight: bfloat16 [2048, 6144], P(None, 'tensor'), may hold values from -0.125 to 0.125
- down_weight: bfloat16 [6144, 2048], P('tensor'), may hold values from -0.078125 to 0.078125
- segment_numbers: int32 [8192], P('dp'), may hold values from 0 to 3, as said below
- positions: int32 [8192], P('dp'), may hold values from 0 to 2047, as said below
- cotangent: bfloat16 [8192, 2048], P('dp'), may hold values from -6 to 6
Outputs:
- layer_output: bfloat16 [8192, 2048], P('dp')
- tokens_gradient: bfloat16 [8192, 2048], P('dp')
- attention_gain_gradient: float32 [2048], P('dp')
- query_gradient: float32 [2048, 2048], P('dp', 'tensor')
- key_gradient: float32 [2048, 1024], P('dp', 'tensor')
- value_gradient: float32 [2048, 1024], P('dp', 'tensor')
- query_gain_gradient: float32 [128], P('dp')
- key_gain_gradient: float32 [128], P('dp')
- output_gradient: float32 [2048, 2048], P('tensor', 'dp')
- feedforward_gain_gradient: float32 [2048], P('dp')
- gate_gradient: float32 [2048, 6144], P('dp', 'tensor')
- up_gradient: float32 [2048, 6144], P('dp', 'tensor')
- down_gradient: float32 [6144, 2048], P('tensor', 'dp')
Inputs may be any that keep to these rules, and one draw needn't show every extreme that they name: `segment_numbers`: each aligned sequence of 1024 tokens holds four documents numbered 0 to 3 in order, never falling, each of 128 tokens or more. `positions`: within a document the position rises by one from token to token; only the first document of a sequence may start at a position above 0, the others start at 0.
All inputs are finite; a program needn't handle non-finite values.
Results may differ from a plain program's by a relative error of at most 0.014.
Values sent between devices are 32-bit elements; how exact they have to be, the bound alone decides.
A program may use at most 256 MiB of HBM per device.

v0:
```python
import functools

import jax
import jax.numpy as jnp
from jax import lax
from jax.experimental import pallas as pl
from jax.experimental.pallas import tpu as pltpu
from jax.sharding import PartitionSpec as P

HD = 128
SEQ_LEN = 1024


epsilon = 1e-06
rope_base = 1000000.0
masked = -1e30


def rms_inverse(value):
    return lax.rsqrt(jnp.mean(value * value, axis=-1, keepdims=True) + epsilon)


def norm_back(upstream, value, inverse, gain):
    scaled = upstream * gain
    return inverse * scaled - value * inverse**3 * jnp.mean(scaled * value, axis=-1, keepdims=True)


def rotary_tables(positions):
    exponent = jnp.arange(0, HD, 2, dtype=jnp.float32) / HD
    frequency = rope_base ** (-exponent)
    phase = positions.astype(jnp.float32)[:, None] * frequency[None, :]
    phase = jnp.concatenate([phase, phase], axis=-1)
    return (jnp.cos(phase), jnp.sin(phase))


def rotate(value, cosine, sine):
    half = value.shape[-1] // 2
    turned = jnp.concatenate([-value[..., half:], value[..., :half]], axis=-1)
    return value * cosine + turned * sine


def rotate_back(upstream, cosine, sine):
    half = upstream.shape[-1] // 2
    moved = upstream * sine
    return upstream * cosine + jnp.concatenate([moved[..., half:], -moved[..., :half]], axis=-1)


def block_scores(query_rows, keys, row_segments, segments, begin):
    scores = jnp.einsum(
        "rkgd,tkd->kgrt", query_rows, keys, preferred_element_type=jnp.float32
    ) * HD ** (-0.5)
    rows = begin + lax.iota(jnp.int32, query_rows.shape[0])
    columns = lax.iota(jnp.int32, keys.shape[0])
    allowed = (row_segments[:, None] == segments[None, :]) & (rows[:, None] >= columns[None, :])
    return jnp.where(allowed[None, None], scores, masked)


def attend(item):
    queries, keys, values, segments = item
    length = queries.shape[0]
    width = min(512, length)
    outputs = []
    totals = []
    for begin in range(0, length, width):
        scores = block_scores(
            queries[begin : begin + width], keys, segments[begin : begin + width], segments, begin
        )
        peak = jnp.max(scores, axis=-1, keepdims=True)
        expons = jnp.exp(scores - peak)
        total = jnp.sum(expons, axis=-1, keepdims=True)
        chance_low = (expons / total).astype(jnp.bfloat16)
        outputs.append(
            jnp.einsum("kgrt,tkd->rkgd", chance_low, values, preferred_element_type=jnp.float32)
        )
        totals.append(peak + jnp.log(total))
    return (jnp.concatenate(outputs, axis=0), jnp.concatenate(totals, axis=2))


def attend_back(item):
    queries, keys, values, segments, totals, upstream = item
    length = queries.shape[0]
    width = min(512, length)
    query_parts = []
    key_grad = jnp.zeros(keys.shape, jnp.float32)
    value_grad = jnp.zeros(values.shape, jnp.float32)
    for begin in range(0, length, width):
        rows = queries[begin : begin + width]
        scores = block_scores(rows, keys, segments[begin : begin + width], segments, begin)
        chance = jnp.exp(scores - totals[:, :, begin : begin + width])
        chance_low = chance.astype(jnp.bfloat16)
        incoming = upstream[begin : begin + width]
        value_grad = value_grad + jnp.einsum(
            "kgrt,rkgd->tkd", chance_low, incoming, preferred_element_type=jnp.float32
        )
        along = jnp.einsum("rkgd,tkd->kgrt", incoming, values, preferred_element_type=jnp.float32)
        center = jnp.sum(along * chance, axis=-1, keepdims=True)
        score_grad = (chance * (along - center)).astype(jnp.bfloat16)
        query_parts.append(
            jnp.einsum("kgrt,tkd->rkgd", score_grad, keys, preferred_element_type=jnp.float32)
            * HD ** (-0.5)
        )
        key_grad = key_grad + jnp.einsum(
            "kgrt,rkgd->tkd", score_grad, rows, preferred_element_type=jnp.float32
        ) * HD ** (-0.5)
    return (jnp.concatenate(query_parts, axis=0), key_grad, value_grad)


def dot(left, right):
    return jnp.dot(left, right, preferred_element_type=jnp.float32)


def dot_back(left, right):
    return jnp.einsum("tc,dc->td", left, right, preferred_element_type=jnp.float32)


def dot_tokens(left, right):
    return jnp.einsum("tm,tn->mn", left, right, preferred_element_type=jnp.float32)


def line_order(high, place):
    steps = {}
    for block in range(high):
        if block > place:
            steps[block] = high - block + place
        elif block < place:
            steps[block] = high - place + block
    return sorted(steps, key=lambda block: (steps[block], block)) + [place]


MESH = pl.DeviceIdType.MESH


def neighbours():
    dp, tensor = lax.axis_index("dp"), lax.axis_index("tensor")
    core = lax.rem(tensor, 2)
    sibling = {"tensor": tensor + 1 - 2 * core}
    facing = {"tensor": lax.rem(tensor + 2, 4)}
    place = dp // 2
    pair = {"dp": dp + 2 * (1 - 2 * lax.rem(place, 2))}
    return core, sibling, facing, pair


def greet(devices):
    barrier = pltpu.get_barrier_semaphore()
    for device in devices:
        pl.semaphore_signal(barrier, inc=1, device_id=device, device_id_type=MESH)
    pl.semaphore_wait(barrier, len(devices))


def loop_rows(count, step, body):
    def run(index, carry):
        body(pl.ds(pl.multiple_of(index * step, step), step))
        return carry

    lax.fori_loop(0, count // step, run, 0)


def sequence_rows(size, core, which, k):
    side = core if which == 0 else 1 - core
    return pl.multiple_of(side * 4 * size + k * size, size)


def remote(source, target, sems, k, device):
    return pltpu.make_async_remote_copy(
        src_ref=source, dst_ref=target, send_sem=sems.at[0, k], recv_sem=sems.at[1, k],
        device_id=device, device_id_type=MESH,
    )


def front_kernel(
    size, first,
    mixed_hbm, output_weight_hbm, tokens_hbm, upstream_hbm, upstream_first,
    gain, gate_hbm, up_hbm, down_hbm,
    hidden_out, second_out, low_own, product_own, gate_own, upward_own,
    low_pair, product_pair, gate_pair, upward_pair, upstream_pair,
    c_landed, n_recv, n_side, u_recv, u_side,
    mixed, output_weight, gate_weight, up_weight, down_weight,
    x_send, x_recv, back_recv, tok, hid, z_send, low, rows16, tiles, stage, terms,
    load_sems, c_sems, x_sems, back_sems, n_sems, n_side_sems, u_sems, u_side_sems,
    tok_sems, hid_sems, low_sems, wave_sems, tile_sems, stage_sems, term_sems,
):
    core, sibling, facing, pair = neighbours()
    depth = gain.shape[1]
    half = 4 * size
    units = gate_weight.shape[1]
    begin = functools.partial(sequence_rows, size, core)
    across_last = (((1,), (1,)), ((), ()))
    rest = half - first
    loads = [
        pltpu.make_async_copy(source, target, load_sems.at[index])
        for index, (source, target) in enumerate(
            [
                (
                    upstream_hbm.at[pl.ds(pl.multiple_of(core * half + first, 16), rest)],
                    rows16.at[pl.ds(0, rest)],
                ),
                (mixed_hbm, mixed),
                (output_weight_hbm, output_weight),
                (gate_hbm, gate_weight),
                (up_hbm, up_weight),
                (down_hbm, down_weight),
            ]
        )
    ]
    for load in loads:
        load.start()
    greet([sibling, facing, pair])

    c_copies = [
        remote(terms.at[pl.ds(k * size, size)], c_landed.at[k], c_sems, k, sibling) for k in range(4)
    ]
    x_copies = [remote(x_send.at[k], x_recv.at[k], x_sems, k, facing) for k in range(4)]
    back_copies = [remote(x_send.at[k], back_recv.at[k], back_sems, k, sibling) for k in range(4)]
    n_copies = [remote(z_send.at[k % 2], n_recv.at[k], n_sems, k, pair) for k in range(4)]
    n_sides = [remote(n_recv.at[k], n_side.at[k], n_side_sems, k, sibling) for k in range(4)]
    u_rows = [(0, rest - 2 * size), (rest - 2 * size, size), (rest - size, size)]
    u_buffers = [hid.at[0, pl.ds(0, u_rows[0][1])], z_send.at[0], z_send.at[1]]
    u_copies = [
        remote(u_buffers[j], u_recv.at[pl.ds(start, number)], u_sems, j, pair)
        for j, (start, number) in enumerate(u_rows)
    ]
    u_sides = [remote(upstream_first, u_side.at[pl.ds(0, first)], u_side_sems, 0, sibling)] + [
        remote(
            u_recv.at[pl.ds(start, number)],
            u_side.at[pl.ds(first + start, number)],
            u_side_sems,
            1 + j,
            sibling,
        )
        for j, (start, number) in enumerate(u_rows)
    ]

    def stage_load(source, slot, number):
        return pltpu.make_async_copy(source, stage.at[slot, pl.ds(0, number)], stage_sems.at[slot])

    def upstream_send(j):
        start, number = u_rows[j]

        def run(row):
            u_buffers[j][row, :] = rows16[
                pl.ds(pl.multiple_of(start + row.start, 16), row.size), :
            ].astype(jnp.float32)

        loop_rows(number, 16, run)
        u_copies[j].start()

    def upstream_forward(j):
        u_copies[j].wait_recv()
        u_sides[1 + j].start()

    def attention_terms(k):
        rows = jnp.concatenate(
            [mixed[pl.ds(begin(which, k), size), :] for which in range(2)], axis=0
        )

        def run(column):
            both = jnp.dot(rows, output_weight[:, column], preferred_element_type=jnp.float32)
            x_send[k, :, column] = both[:size]
            terms[pl.ds(k * size, size), column] = both[size:]

        loop_rows(depth, 1024, run)
        c_copies[k].start()

    def attention_cores(k):
        c_copies[k].wait_recv()
        stage_load(c_landed.at[k], k % 2, size).start()
        stage_load(c_landed.at[k], k % 2, size).wait()

        def run(row):
            x_send[k, row, :] = x_send[k, row, :] + stage[k % 2, row, :]

        loop_rows(size, 16, run)
        x_copies[k].start()

    def attention_chips(k):
        x_copies[k].wait()

        def run(row):
            x_send[k, row, :] = x_send[k, row, :] + x_recv[k, row, :]

        loop_rows(size, 16, run)
        back_copies[k].start()

    def token_loads(k):
        return [
            pltpu.make_async_copy(
                tokens_hbm.at[pl.ds(begin(which, k), size)], tok.at[which], tok_sems.at[which]
            )
            for which in range(2)
        ]

    def hidden_stores(k):
        return [
            pltpu.make_async_copy(
                hid.at[which], hidden_out.at[pl.ds(begin(which, k), size)], hid_sems.at[which]
            )
            for which in range(2)
        ]

    def low_rows(which, k, row):
        side = core if which == 0 else 1 - core
        return pl.ds(pl.multiple_of((side + k % 2 * 2) * size + row.start, 16), row.size)

    def normed(k):
        for load in token_loads(k):
            load.wait()
        if k > 0:
            for store in hidden_stores(k - 1):
                store.wait()
        if k < 2:
            u_copies[1 + k].wait_send()
        else:
            n_copies[k - 2].wait_send()

        def run(which, source, row):
            value = tok[which, row, :].astype(jnp.float32) + source[k, row, :]
            hid[which, row, :] = value
            unit = value * lax.rsqrt(jnp.mean(value * value, axis=-1, keepdims=True) + epsilon)
            if which == 0:
                z_send[k % 2, row, :] = unit
            low[0, low_rows(which, k, row), :] = (unit * gain[...]).astype(jnp.bfloat16)

        loop_rows(size, 16, functools.partial(run, 0, x_send))
        n_copies[k].start()
        back_copies[k].wait_recv()
        loop_rows(size, 16, functools.partial(run, 1, back_recv))
        for store in hidden_stores(k):
            store.start()
        if k < 3:
            for load in token_loads(k + 1):
                load.start()

    def pipeline(pieces):
        def bring(index):
            before, source, number, _ = pieces[index]
            if before is not None:
                before.wait_recv()
            stage_load(source, index % 2, number).start()

        bring(0)
        for index, (_, source, number, consume) in enumerate(pieces):
            if index + 1 < len(pieces):
                bring(index + 1)
            stage_load(source, index % 2, number).wait()
            loop_rows(number, 16, functools.partial(consume, index % 2))

    def pair_forward(k):
        n_copies[k].wait_recv()
        n_sides[k].start()

    def pair_rows(chunks):
        def consume(k, which, slot, row):
            low[1, low_rows(which, k, row), :] = (stage[slot, row, :] * gain[...]).astype(
                jnp.bfloat16
            )

        pipeline(
            [
                (
                    n_sides[k] if which else None,
                    (n_side if which else n_recv).at[k],
                    size,
                    functools.partial(consume, k, which),
                )
                for which in range(2)
                for k in chunks
            ]
        )

    def wave_copies(local, distant, sems, wave, inwards=False):
        copies = []
        for part in range(4):
            here = local.at[pl.ds(part * size, size)]
            there = distant.at[pl.ds(part % 2 * half + (2 * wave + part // 2) * size, size)]
            source, target = (there, here) if inwards else (here, there)
            copies.append(pltpu.make_async_copy(source, target, sems.at[part]))
        return copies

    def pair_stores(wave):
        return wave_copies(rows16, upstream_pair, wave_sems.at[1], wave)

    def upstream_wave(wave):
        def consume(which, start, slot, row):
            side = core if which == 0 else 1 - core
            chunk, within = start // size, start % size
            place = pl.multiple_of((2 * chunk + side) * size + within + row.start, 16)
            rows16[pl.ds(place, row.size), :] = stage[slot, row, :].astype(jnp.bfloat16)

        if wave == 0:
            own = [
                (upstream_first.at[pl.ds(0, size)], size, 0),
                (upstream_first.at[pl.ds(size, first - size)], first - size, size),
                (u_recv.at[pl.ds(0, u_rows[0][1])], u_rows[0][1], first),
            ]
            waits = [u_sides[0], u_sides[1]]
        else:
            own = [(u_recv.at[pl.ds(u_rows[j][0], size)], size, (j - 1) * size) for j in (1, 2)]
            waits = [u_sides[2], u_sides[3]]
        pieces = [
            (None, source, number, functools.partial(consume, 0, start))
            for source, number, start in own
        ]
        if wave == 0:
            waits[0].wait_recv()
            waits[1].wait_recv()
            waits = [None, None]
        pieces += [
            (
                waits[j],
                u_side.at[pl.ds((2 * wave + j) * size, size)],
                size,
                functools.partial(consume, 1, j * size),
            )
            for j in range(2)
        ]
        pipeline(pieces)
        for copy in pair_stores(wave):
            copy.start()

    def term_stores(wave):
        return wave_copies(terms, second_out, term_sems, wave)

    def low_stores(wave, index):
        return wave_copies(low.at[index], low_pair if index else low_own, low_sems.at[index], wave)

    def tile_stores(wave, index):
        outs = (
            (product_pair, gate_pair, upward_pair) if index else (product_own, gate_own, upward_own)
        )
        return [
            copy
            for which in range(3)
            for copy in wave_copies(tiles.at[which], outs[which], tile_sems.at[which], wave)
        ]

    feeds = [(0, 0), (0, 1), (1, 0), (1, 1)]

    def fetches(wave):
        return wave_copies(rows16, upstream_hbm, wave_sems.at[0], wave, True)

    def feed(wave, index, part=None):
        number = feeds.index((wave, index))
        rows = slice(None) if part is None else pl.ds(part * 2 * size, 2 * size)
        if not part:
            if number > 0:
                for copy in tile_stores(*feeds[number - 1]):
                    copy.wait()
        if index == 0:
            for copy in fetches(wave):
                copy.wait()

        def run(column):
            gate = jnp.dot(
                low[index, rows], gate_weight[:, column], preferred_element_type=jnp.float32
            )
            upward = jnp.dot(
                low[index, rows], up_weight[:, column], preferred_element_type=jnp.float32
            )
            grad = lax.dot_general(
                rows16[rows],
                down_weight[column, :],
                across_last,
                preferred_element_type=jnp.float32,
            )
            sigmoid_gate = jax.nn.sigmoid(gate)
            activated = gate * sigmoid_gate
            tiles[0, rows, column] = (activated * upward).astype(jnp.bfloat16)
            tiles[1, rows, column] = (
                grad * upward * sigmoid_gate * (1.0 + gate * (1.0 - sigmoid_gate))
            ).astype(jnp.bfloat16)
            tiles[2, rows, column] = (grad * activated).astype(jnp.bfloat16)

        loop_rows(units, 512, run)
        copies = tile_stores(wave, index) + low_stores(wave, index)
        for number, copy in enumerate(copies):
            if part is None or number % 4 // 2 == part:
                copy.start()
        if index == 0:
            if wave > 0:
                for copy in term_stores(wave - 1):
                    copy.wait()

            def second(column):
                terms[:, column] = lax.dot_general(
                    tiles[1],
                    gate_weight[column, :],
                    across_last,
                    preferred_element_type=jnp.float32,
                ) + lax.dot_general(
                    tiles[2],
                    up_weight[column, :],
                    across_last,
                    preferred_element_type=jnp.float32,
                )

            loop_rows(depth, 512, second)
            for copy in term_stores(wave):
                copy.start()

    for load in token_loads(0):
        load.start()
    loads[0].wait()
    for j in range(3):
        upstream_send(j)
    u_sides[0].start()
    loads[1].wait()
    loads[2].wait()
    attention_terms(0)
    attention_terms(1)
    attention_cores(0)
    attention_terms(2)
    attention_cores(1)
    attention_terms(3)
    attention_cores(2)
    attention_cores(3)
    for copy in fetches(0):
        copy.start()
    upstream_forward(0)
    attention_chips(0)
    u_copies[0].wait_send()
    upstream_forward(1)
    normed(0)
    for load in loads[3:]:
        load.wait()
    attention_chips(1)
    normed(1)
    upstream_forward(2)
    for k in range(4):
        c_copies[k].wait_send()
    feed(0, 0)
    attention_chips(2)
    for copy in low_stores(0, 0):
        copy.wait()
    normed(2)
    pair_forward(0)
    upstream_wave(0)
    attention_chips(3)
    normed(3)
    pair_forward(1)
    pair_rows((0, 1))
    feed(0, 1)
    for copy in pair_stores(0):
        copy.wait()
    for copy in fetches(1):
        copy.start()
    pair_forward(2)
    feed(1, 0)
    upstream_wave(1)
    for copy in low_stores(0, 1):
        copy.wait()
    pair_rows((2,))
    feed(1, 1, 0)
    pair_forward(3)
    pair_rows((3,))
    feed(1, 1, 1)

    for k in range(4):
        back_copies[k].wait_send()
        n_sides[k].wait_send()
        u_sides[k].wait_send()
        if k >= 2:
            n_copies[k].wait_send()
    ends = hidden_stores(3) + term_stores(1) + low_stores(1, 0) + low_stores(1, 1)
    for copy in ends + pair_stores(1) + tile_stores(1, 1):
        copy.wait()


def front(mixed, output_weight, tokens, upstream, upstream_first, gain, gate_weight, up_weight, down_weight):
    rows, depth = tokens.shape
    inner, units = mixed.shape[1], gate_weight.shape[1]
    first = upstream_first.shape[0]
    size = rows // 8
    f32, b16 = jnp.float32, jnp.bfloat16
    any_space = pl.BlockSpec(memory_space=pl.ANY)
    shape = jax.ShapeDtypeStruct
    outs = [shape((rows, depth), f32)] * 2
    outs += ([shape((rows, depth), b16)] + [shape((rows, units), b16)] * 3) * 2
    outs += [shape((rows, depth), b16)] + [shape((4, size, depth), f32)] * 3
    outs += [shape((4 * size - first, depth), f32), shape((4 * size, depth), f32)]
    dma = pltpu.SemaphoreType.DMA
    vmem = pltpu.VMEM
    return pl.pallas_call(
        functools.partial(front_kernel, size, first),
        out_shape=outs,
        in_specs=[any_space] * 5 + [pl.BlockSpec(memory_space=pltpu.VMEM)] + [any_space] * 3,
        out_specs=[any_space] * len(outs),
        scratch_shapes=[
            vmem((rows, inner), b16),
            vmem((inner, depth), b16),
            vmem((depth, units), b16),
            vmem((depth, units), b16),
            vmem((units, depth), b16),
            vmem((4, size, depth), f32),
            vmem((4, size, depth), f32),
            vmem((4, size, depth), f32),
            vmem((2, size, depth), b16),
            vmem((2, size, depth), f32),
            vmem((2, size, depth), f32),
            vmem((2, 4 * size, depth), b16),
            vmem((4 * size, depth), b16),
            vmem((3, 4 * size, units), b16),
            vmem((2, size, depth), f32),
            vmem((4 * size, depth), f32),
            dma((6,)),
            *[dma((2, 4))] * 5,
            dma((2, 3)),
            dma((2, 4)),
            dma((2,)),
            dma((2,)),
            dma((2, 4)),
            dma((2, 4)),
            dma((3, 4)),
            dma((2,)),
            dma((4,)),
        ],
        compiler_params=pltpu.CompilerParams(
            collective_id=1, has_side_effects=True, vmem_limit_bytes=63 * 1024 * 1024
        ),
        cost_estimate=pl.CostEstimate(
            flops=12 * rows * depth * units, bytes_accessed=6 * depth * units, transcendentals=0
        ),
    )(mixed, output_weight, tokens, upstream, upstream_first, gain[None], gate_weight, up_weight, down_weight)


def grid_neighbours():
    dp = lax.axis_index("dp")
    place, lane = dp // 2, lax.rem(dp, 2)
    towards = 1 - 2 * (place // 2)
    across = {"dp": dp + 1 - 2 * lane}
    inward, outward = {"dp": dp + 2 * towards}, {"dp": dp - 2 * towards}
    team = place // 2
    side = lax.rem(place, 2)
    inner = lax.rem(team + side, 2)
    return place, lane, team, side, inner, across, inward, outward


def greet_grid(always, inner, outward):
    barrier = pltpu.get_barrier_semaphore()
    for device in always:
        pl.semaphore_signal(barrier, inc=1, device_id=device, device_id_type=MESH)

    @pl.when(inner == 1)
    def _():
        pl.semaphore_signal(barrier, inc=1, device_id=outward, device_id_type=MESH)

    pl.semaphore_wait(barrier, len(always) + inner)


def middle_kernel(
    size,
    second_hbm, hidden_hbm, upstream_hbm, upstream_pair, product_own, product_pair,
    gate_own, gate_pair, low_own, low_pair, gain, down_hbm,
    grad_out, grad_low_out, out_part, weight_out, gate_ready, gate_given, gate_own_block,
    products, down_weight, columns, c_recv, x_send, x_recv, back_recv,
    y_send, y_recv, kept, in_recv, mid_recv, out_recv,
    hid, tok, grad, grad_low, out_stage, gate_send, gate_kept, gate_stage,
    load_sems, gate_load_sems, gate_sems, c_sems, x_sems, back_sems, y_sems, z_sems, column_sems,
    x_load_sems, hid_sems, tok_sems, grad_sems, low_sems, out_sems, weight_sems,
):
    core, sibling, facing, _ = neighbours()
    place, lane, team, side, inner, across, inward, outward = grid_neighbours()
    depth = gain.shape[1]
    units = down_weight.shape[0]
    width = columns.shape[-1]
    begin = functools.partial(sequence_rows, size, core)
    rows_in = 8 * size
    down_first = (((0,), (0,)), ((), ()))
    loads = [
        pltpu.make_async_copy(source, target, load_sems.at[index])
        for index, (source, target) in enumerate(
            [
                (product_own, products.at[pl.ds(0, rows_in)]),
                (product_pair, products.at[pl.ds(rows_in, rows_in)]),
                (down_hbm, down_weight),
            ]
        )
    ]
    gate_loads = [
        pltpu.make_async_copy(
            source, products.at[pl.ds(index * rows_in, rows_in)], gate_load_sems.at[index]
        )
        for index, source in enumerate((gate_own, gate_pair))
    ]
    turns = [(0, 1), (1, 1), (0, 0), (1, 0)]
    turns += [(0, 1), (1, 1), (1, 0), (0, 0)]

    def column_loads(index):
        turn, other = turns[index]
        spot = lax.rem(1 - team + turn, 2)
        which = 1 - lane if other else lane
        start = pl.multiple_of((side * 4 + 2 * spot + which) * width, width)
        return [
            pltpu.make_async_copy(
                source.at[:, pl.ds(start, width)],
                columns.at[index % 2, pl.ds(part * rows_in, rows_in)],
                column_sems.at[index % 2, part],
            )
            for part, source in enumerate(
                (upstream_hbm, upstream_pair) if index < 4 else (low_own, low_pair)
            )
        ]

    x_loads = [
        pltpu.make_async_copy(
            second_hbm.at[pl.ds(begin(0, k), size)], x_send.at[k], x_load_sems.at[k]
        )
        for k in range(4)
    ]
    for copy in column_loads(0) + x_loads[:1] + loads[:2] + column_loads(1) + x_loads[1:] + loads[2:]:
        copy.start()
    greet_grid([sibling, facing, across, inward], inner, outward)
    c_copies = [
        remote(second_hbm.at[pl.ds(begin(1, k), size)], c_recv.at[k], c_sems, k, sibling)
        for k in range(4)
    ]
    x_copies = [remote(x_send.at[k], x_recv.at[k], x_sems, k, facing) for k in range(4)]
    back_copies = [remote(x_send.at[k], back_recv.at[k], back_sems, k, sibling) for k in range(4)]
    y_copies = [remote(y_send.at[k], y_recv.at[k], y_sems, k, across) for k in range(2)]
    in_copy = remote(kept.at[0], in_recv, z_sems, 0, inward)
    mid_copies = [remote(kept.at[k], mid_recv.at[k], z_sems, 1 + k, inward) for k in range(2)]
    out_copy = remote(mid_recv.at[0], out_recv, z_sems, 3, outward)
    for copy in c_copies:
        copy.start()

    def cores(k):
        x_loads[k].wait()
        c_copies[k].wait_recv()

        def run(row):
            x_send[k, row, :] = x_send[k, row, :] + c_recv[k, row, :]

        loop_rows(size, 16, run)
        x_copies[k].start()

    def chips(k):
        x_copies[k].wait()

        def run(row):
            x_send[k, row, :] = x_send[k, row, :] + x_recv[k, row, :]

        loop_rows(size, 16, run)
        back_copies[k].start()

    def block(index, target):
        for copy in column_loads(index):
            copy.wait()

        target[...] = lax.dot_general(
            products[...], columns[index % 2], down_first, preferred_element_type=jnp.float32
        )
        for copy in column_loads(index + 2):
            copy.start()

    gate_copy = remote(gate_send, gate_kept, gate_sems, 0, across)

    def gate_block(index, target):
        for copy in column_loads(index):
            copy.wait()
        target[...] = lax.dot_general(
            columns[index % 2], products[...], down_first, preferred_element_type=jnp.float32
        )
        if index + 2 < len(turns):
            for copy in column_loads(index + 2):
                copy.start()

    def gate_store(source, target, index):
        return pltpu.make_async_copy(source, target, gate_load_sems.at[2 + index])

    def chunk_loads(k):
        return [
            pltpu.make_async_copy(
                source.at[pl.ds(begin(which, k), size)], target.at[which], sems.at[which]
            )
            for which in range(2)
            for source, target, sems in ((hidden_hbm, hid, hid_sems), (upstream_hbm, tok, tok_sems))
        ]

    def grad_stores(k):
        return [
            pltpu.make_async_copy(
                source.at[which], target.at[pl.ds(begin(which, k), size)], sems.at[which]
            )
            for which in range(2)
            for source, target, sems in (
                (grad, grad_out, grad_sems),
                (grad_low, grad_low_out, low_sems),
            )
        ]

    def finish(k):
        for copy in chunk_loads(k):
            copy.wait()
        if k > 0:
            for copy in grad_stores(k - 1):
                copy.wait()
        back_copies[k].wait_recv()

        def run(which, source, row):
            value = hid[which, row, :]
            inverse = lax.rsqrt(jnp.mean(value * value, axis=-1, keepdims=True) + epsilon)
            total = tok[which, row, :].astype(jnp.float32) + norm_back(
                source[k, row, :], value, inverse, gain[...]
            )
            grad[which, row, :] = total
            grad_low[which, row, :] = total.astype(jnp.bfloat16)

        for which, source in enumerate((x_send, back_recv)):
            loop_rows(size, 16, functools.partial(run, which, source))
        for copy in grad_stores(k):
            copy.start()
        if k < 3:
            for copy in chunk_loads(k + 1):
                copy.start()

    def out_store(k):
        rows = 2 * size
        return pltpu.make_async_copy(
            out_stage, out_part.at[pl.ds(k * rows, rows)], out_sems.at[0]
        )

    def out_terms(k):
        if k > 0:
            out_store(k - 1).wait()
        rows = pl.ds(k * 2 * size, 2 * size)

        def run(column):
            out_stage[:, column] = jnp.dot(
                products[rows, :], down_weight[:, column], preferred_element_type=jnp.float32
            )

        loop_rows(depth, 1024, run)
        out_store(k).start()

    def take(k):
        y_copies[k].wait_recv()

        def run(row):
            kept[k, row, :] = kept[k, row, :] + y_recv[k, row, :]

        loop_rows(units, 64, run)

    for copy in loads[:2]:
        copy.wait()
    block(0, y_send.at[0])
    y_copies[0].start()
    cores(0)
    for copy in chunk_loads(0):
        copy.start()
    cores(1)
    cores(2)
    cores(3)
    block(1, y_send.at[1])
    y_copies[1].start()
    block(2, kept.at[0])
    loads[2].wait()
    out_terms(0)
    chips(0)
    out_terms(1)
    block(3, kept.at[1])
    finish(0)
    out_terms(2)
    take(0)

    @pl.when(inner == 1)
    def _():
        mid_copies[0].start()

    @pl.when(inner == 0)
    def _():
        in_copy.start()

    out_terms(3)
    for copy in gate_loads:
        copy.start()
    chips(1)
    for copy in gate_loads:
        copy.wait()
    gate_block(4, gate_send)
    gate_copy.start()
    finish(1)
    gate_block(5, gate_stage)
    gate_store(gate_stage, gate_given, 0).start()
    chips(2)
    take(1)

    @pl.when(inner == 1)
    def _():
        mid_copies[1].start()
        mid_copies[0].wait_recv()
        out_copy.start()

    finish(2)
    gate_store(gate_stage, gate_given, 0).wait()
    gate_block(6, gate_stage)
    gate_store(gate_stage, gate_own_block, 1).start()
    gate_store(gate_stage, gate_own_block, 1).wait()
    gate_block(7, gate_stage)
    chips(3)
    finish(3)
    gate_copy.wait()

    def run_gate(row):
        gate_kept[row, :] = gate_kept[row, :] + gate_stage[row, :]

    loop_rows(width, 16, run_gate)
    gate_store(gate_kept, gate_ready, 2).start()

    @pl.when(inner == 1)
    def _():
        in_copy.wait_recv()
        mid_copies[1].wait_recv()
        mid_copies[0].wait_send()
        mid_copies[1].wait_send()
        out_copy.wait_send()

        def run(row):
            kept[0, row, :] = in_recv[row, :] + mid_recv[1, row, :]

        loop_rows(units, 64, run)

    @pl.when(inner == 0)
    def _():
        in_copy.wait_send()
        out_copy.wait_recv()

        def run(row):
            kept[0, row, :] = kept[1, row, :] + out_recv[row, :]

        loop_rows(units, 64, run)

    store = pltpu.make_async_copy(kept.at[0], weight_out, weight_sems.at[0])
    store.start()
    for k in range(4):
        back_copies[k].wait_send()
        c_copies[k].wait_send()
    for k in range(2):
        y_copies[k].wait_send()
    for copy in grad_stores(3):
        copy.wait()
    gate_store(gate_kept, gate_ready, 2).wait()
    out_store(3).wait()
    store.wait()


def middle(
    second, hidden, upstream, upstream_pair, product_own, product_pair,
    gate_own, gate_pair, low_own, low_pair, gain, down_weight,
):
    rows, depth = hidden.shape
    units = down_weight.shape[0]
    size = rows // 8
    width = depth // 8
    f32, b16 = jnp.float32, jnp.bfloat16
    any_space = pl.BlockSpec(memory_space=pl.ANY)
    shape = jax.ShapeDtypeStruct
    dma = pltpu.SemaphoreType.DMA
    vmem = pltpu.VMEM
    return pl.pallas_call(
        functools.partial(middle_kernel, size),
        out_shape=[
            shape((rows, depth), f32),
            shape((rows, depth), b16),
            shape((rows, depth), f32),
            shape((units, width), f32),
        ]
        + [shape((width, units), f32)] * 3,
        in_specs=[any_space] * 10 + [pl.BlockSpec(memory_space=pltpu.VMEM), any_space],
        out_specs=[any_space] * 7,
        scratch_shapes=[
            vmem((2 * rows, units), b16),
            vmem((units, depth), b16),
            vmem((2, 2 * rows, width), b16),
            vmem((4, size, depth), f32),
            vmem((4, size, depth), f32),
            vmem((4, size, depth), f32),
            vmem((4, size, depth), f32),
            vmem((2, units, width), f32),
            vmem((2, units, width), f32),
            vmem((2, units, width), f32),
            vmem((units, width), f32),
            vmem((2, units, width), f32),
            vmem((units, width), f32),
            vmem((2, size, depth), f32),
            vmem((2, size, depth), b16),
            vmem((2, size, depth), f32),
            vmem((2, size, depth), b16),
            vmem((2 * size, depth), f32),
            vmem((width, units), f32),
            vmem((width, units), f32),
            vmem((width, units), f32),
            dma((3,)),
            dma((5,)),
            dma((2, 1)),
            dma((2, 4)),
            dma((2, 4)),
            dma((2, 4)),
            dma((2, 2)),
            dma((2, 4)),
            dma((2, 2)),
            dma((4,)),
            dma((2,)),
            dma((2,)),
            dma((2,)),
            dma((2,)),
            dma((1,)),
            dma((1,)),
        ],
        compiler_params=pltpu.CompilerParams(
            collective_id=2, has_side_effects=True, vmem_limit_bytes=62 * 1024 * 1024
        ),
        cost_estimate=pl.CostEstimate(
            flops=8 * rows * depth * units, bytes_accessed=6 * depth * units, transcendentals=0
        ),
    )(
        second, hidden, upstream, upstream_pair, product_own, product_pair,
        gate_own, gate_pair, low_own, low_pair, gain[None], down_weight,
    )


class TensorSum:
    def __init__(self, size, own, landed, stage, sems, stage_sems, devices):
        self.size, self.own, self.landed, self.stage = size, own, landed, stage
        self.stage_sems = stage_sems
        c_sems, x_sems, back_sems = sems
        self.sibling, facing = devices
        self.c_sems = c_sems
        self.x_copies = [remote(own.at[k], landed[1].at[k], x_sems, k, facing) for k in range(4)]
        self.back_copies = [
            remote(own.at[k], landed[2].at[k], back_sems, k, self.sibling) for k in range(4)
        ]
        self.c_copies = [None] * 4

    def give(self, k, source):
        self.c_copies[k] = remote(source, self.landed[0].at[k], self.c_sems, k, self.sibling)
        self.c_copies[k].start()

    def staged(self, which, k):
        copy = pltpu.make_async_copy(self.landed[which].at[k], self.stage.at[0], self.stage_sems.at[0])
        copy.start()
        copy.wait()

    def add_stage(self, k):
        def run(row):
            self.own[k, row, :] = self.own[k, row, :] + self.stage[0, row, :]

        loop_rows(self.size, 16, run)

    def cores(self, k):
        self.c_copies[k].wait_recv()
        self.staged(0, k)
        self.add_stage(k)
        self.x_copies[k].start()

    def chips(self, k):
        self.x_copies[k].wait()
        self.staged(1, k)
        self.add_stage(k)
        self.back_copies[k].start()

    def other(self, k):
        self.back_copies[k].wait_recv()
        self.staged(2, k)


def rear_kernel(
    size, turns,
    gate_middle, gate_inward, gate_ready, low_own, low_pair, upward_own, upward_pair,
    normed_hbm, raw_hbm, hidden_low_hbm, mixed_hbm, lines,
    out_hbm, hidden_hbm, grad_hbm, tokens_hbm,
    query_hbm, key_hbm, value_hbm, gate_hbm, up_hbm, gain, feed_gain,
    layer_out, tokens_out, gate_out, up_out, raw_out, head_out, gains_out,
    o_c, o_x, o_back, d_c, d_x, d_back, gate_landed, up_landed,
    upwards, raw, mixed, head_weights, feed_rows, gains, gain_rows, gains_in, columns,
    up_send, up_kept, raw_send, raw_kept, head_send, head_kept, raw_line, head_line,
    own, give, stage, wide, narrow, result,
    load_sems, column_sems, y_up_sems, y_raw_sems, y_head_sems, gate_sems, up_sems,
    raw_line_sems, head_line_sems,
    oc_sems, ox_sems, ob_sems, dc_sems, dx_sems, db_sems,
    own_sems, stage_sems, wide_sems, narrow_sems, result_sems, end_sems, gain_sems,
):
    core, sibling, facing, _ = neighbours()
    place, lane, team, side, inner, across, inward, outward = grid_neighbours()
    high = len(turns)
    depth = gain.shape[1]
    width = columns.shape[-1]
    units = upwards.shape[-1]
    begin = functools.partial(sequence_rows, size, core)
    rows_in = 8 * size
    down_first = (((0,), (0,)), ((), ()))
    cuts = (query_hbm.shape[1], key_hbm.shape[1])
    own_rows = pl.ds(pl.multiple_of(lax.axis_index("dp") * width, width), width)
    loads = [
        pltpu.make_async_copy(source, target, load_sems.at[index])
        for index, (source, target) in enumerate(
            [
                (raw_hbm, raw),
                (mixed_hbm, mixed),
                (upward_own, upwards.at[pl.ds(0, rows_in)]),
                (upward_pair, upwards.at[pl.ds(rows_in, rows_in)]),
                (query_hbm, head_weights.at[:, pl.ds(0, cuts[0])]),
                (key_hbm, head_weights.at[:, pl.ds(cuts[0], cuts[1])]),
                (value_hbm, head_weights.at[:, pl.ds(cuts[0] + cuts[1], cuts[1])]),
                (gate_hbm.at[own_rows], feed_rows.at[0]),
                (up_hbm.at[own_rows], feed_rows.at[1]),
            ]
        )
    ]
    blocks = [
        ("head", 0, 1), ("up", 0, 1), ("up", 1, 1), ("head", 1, 1), ("head", 2, 1), ("head", 3, 1),
        ("head", 0, 0), ("up", 0, 0), ("up", 1, 0), ("head", 1, 0), ("head", 2, 0), ("head", 3, 0),
    ]

    def spot_of(kind, turn):
        if kind == "up":
            return side * 2 + lax.rem(1 - team + turn, 2)
        spot = jnp.int32(turns[0][turn])
        for p in range(1, high):
            spot = jnp.where(place == p, jnp.int32(turns[p][turn]), spot)
        return spot

    def column_loads(index):
        kind, turn, other = blocks[index]
        which = 1 - lane if other else lane
        start = pl.multiple_of((2 * spot_of(kind, turn) + which) * width, width)
        sources = (low_own, low_pair) if kind == "up" else (normed_hbm, hidden_low_hbm)
        return [
            pltpu.make_async_copy(
                source.at[:, pl.ds(start, width)],
                columns.at[index % 2, pl.ds(part * rows_in, rows_in)],
                column_sems.at[index % 2, part],
            )
            for part, source in enumerate(sources)
        ]

    own_loads = [
        pltpu.make_async_copy(out_hbm.at[pl.ds(begin(0, k), size)], own.at[k], own_sems.at[k])
        for k in range(4)
    ]
    for copy in column_loads(0) + loads[:2] + column_loads(1) + own_loads + loads[2:]:
        copy.start()
    greet_grid([sibling, facing, across, inward], inner, outward)
    devices = (sibling, facing)
    outs = TensorSum(
        size, own, (o_c, o_x, o_back), stage, (oc_sems, ox_sems, ob_sems), stage_sems, devices
    )
    heads = TensorSum(
        size, own, (d_c, d_x, d_back), stage, (dc_sems, dx_sems, db_sems), stage_sems, devices
    )
    for k in range(4):
        outs.give(k, out_hbm.at[pl.ds(begin(1, k), size)])

    def team_copies(values, landed, sems):
        return (
            remote(values[0], landed.at[0], sems, 0, inward),
            [remote(values[k], landed.at[1 + k], sems, 1 + k, inward) for k in range(2)],
            remote(landed.at[1], landed.at[3], sems, 3, outward),
        )

    gate_copies = (
        None,
        [None, remote(gate_ready, gate_landed.at[0], gate_sems, 0, inward)],
        remote(gate_middle, gate_landed.at[1], gate_sems, 1, outward),
    )
    up_copies = team_copies((up_kept.at[0], up_kept.at[1]), up_landed, up_sems)

    def team_send(copies, turn):
        @pl.when(inner == 1)
        def _():
            copies[1][turn].start()

        if turn == 0:

            @pl.when(inner == 0)
            def _():
                copies[0].start()

    def team_forward(copies):
        @pl.when(inner == 1)
        def _():
            copies[1][0].wait_recv()
            copies[2].start()

    def add_gain(lane_index, row, value, weight):
        total = jnp.sum(value * weight.astype(jnp.float32), axis=-1, keepdims=True)
        lanes = lax.broadcasted_iota(jnp.int32, (total.shape[0], gains.shape[1]), 1)
        gains[row, :] = gains[row, :] + jnp.where(lanes == lane_index, total, 0.0)

    def team_combine(copies, first, second, outward_landed, last, out, sem, which):
        def fetch(source, slot):
            copy = pltpu.make_async_copy(source, up_send.at[slot], end_sems.at[4 + slot])
            copy.start()
            copy.wait()

        @pl.when(inner == 1)
        def _():
            if copies[0] is not None:
                copies[0].wait_recv()
                copies[1][0].wait_send()
            copies[1][1].wait_recv()
            fetch(first, 0)
            fetch(second, 1)
            copies[1][1].wait_send()
            copies[2].wait_send()

        @pl.when(inner == 0)
        def _():
            if copies[0] is not None:
                copies[0].wait_send()
            copies[2].wait_recv()
            fetch(outward_landed, 0)
            fetch(last, 1)

        def run(row):
            total = up_send[0, row, :] + up_send[1, row, :]
            up_send[0, row, :] = total
            add_gain(1, row, total, feed_rows[which, row, :])

        loop_rows(width, 16, run)
        store = pltpu.make_async_copy(up_send.at[0], out, sem)
        store.start()
        store.wait()

    y_up = [remote(up_send.at[k], up_kept.at[k], y_up_sems, k, across) for k in range(2)]
    y_raw = [remote(raw_send.at[k], raw_kept.at[k], y_raw_sems, k, across) for k in range(high)]
    y_head = [
        remote(head_send.at[k], head_kept.at[k], y_head_sems, k, across) for k in range(high)
    ]

    def line_copy(p, turn, towards=None):
        block = turns[p][turn]
        ahead = block > p
        slot = block - 1 if ahead else high - 1 + block
        device = {"dp": lax.axis_index("dp") + (2 if ahead else -2)}
        return slot, [
            remote(kept.at[turn], line.at[slot], sems, slot, device)
            for kept, line, sems in (
                (raw_kept, raw_line, raw_line_sems),
                (head_kept, head_line, head_line_sems),
            )
        ]

    def line_arrived(slot, turn):
        for kept, line, sems in (
            (raw_kept, raw_line, raw_line_sems),
            (head_kept, head_line, head_line_sems),
        ):
            remote(kept.at[turn], line.at[slot], sems, slot, across).wait_recv()

            def run(row):
                kept[turn, row, :] = kept[turn, row, :] + line[slot, row, :]

            loop_rows(kept.shape[1], 8, run)

    def line_step(turn):
        for p in range(high):
            block = turns[p][turn]

            @pl.when(place == p)
            def _():
                slot, copies = line_copy(p, turn)
                if (block > p and p > 0) or (block < p and p < high - 1):
                    line_arrived(slot, turn)
                for copy in copies:
                    copy.start()

    def line_end():
        for p in range(high):

            @pl.when(place == p)
            def _():
                if p > 0:
                    line_arrived(p - 1, high - 1)
                if p < high - 1:
                    line_arrived(high - 1 + p, high - 1)
                for turn in range(high - 1):
                    for copy in line_copy(p, turn)[1]:
                        copy.wait_send()

    def up_block(index, target, added):
        for copy in column_loads(index):
            copy.wait()

        total = lax.dot_general(
            columns[index % 2], upwards[...], down_first, preferred_element_type=jnp.float32
        )
        target[...] = target[...] + total if added else total
        if index + 2 < len(blocks):
            for copy in column_loads(index + 2):
                copy.start()

    def head_block(index, raw_target, head_target, added):
        kind, turn, other = blocks[index]
        which = 1 - lane if other else lane
        for copy in column_loads(index):
            copy.wait()
        slot = index % 2
        total = lax.dot_general(
            columns[slot, :rows_in], raw[...], down_first, preferred_element_type=jnp.float32
        )
        line = lines[2 * spot_of(kind, turn) + which]
        raw_target[:width, :] = raw_target[:width, :] + total if added else total
        raw_target[width:, :] = raw_target[width:, :] + line if added else line
        total = lax.dot_general(
            mixed[...], columns[slot, rows_in:], down_first, preferred_element_type=jnp.float32
        )
        head_target[...] = head_target[...] + total if added else total
        if index + 2 < len(blocks):
            for copy in column_loads(index + 2):
                copy.start()

    def head_send_block(index):
        turn = blocks[index][1]
        head_block(index, raw_send.at[turn], head_send.at[turn], False)
        y_raw[turn].start()
        y_head[turn].start()

    def head_take(index):
        turn = blocks[index][1]
        y_raw[turn].wait_recv()
        y_head[turn].wait_recv()
        head_block(index, raw_kept.at[turn], head_kept.at[turn], True)

    def head_terms(k):
        outs.back_copies[k].wait_send()
        if k >= 2:
            heads.c_copies[k - 2].wait_send()
        rows = jnp.concatenate(
            [raw[pl.ds(begin(which, k), size), :] for which in range(2)], axis=0
        )

        def run(column):
            total = lax.dot_general(
                rows,
                head_weights[column, :],
                (((1,), (1,)), ((), ())),
                preferred_element_type=jnp.float32,
            )
            own[k, :, column] = total[:size]
            give[k % 2, :, column] = total[size:]

        loop_rows(depth, 1024, run)
        heads.give(k, give.at[k % 2])

    def fetches(what, k):
        pairs = ((hidden_hbm, wide, wide_sems),)
        if what == "tokens":
            pairs = ((grad_hbm, wide, wide_sems), (tokens_hbm, narrow, narrow_sems))
        return [
            pltpu.make_async_copy(
                source.at[pl.ds(begin(which, k), size)], target.at[which], sems.at[which]
            )
            for which in range(2)
            for source, target, sems in pairs
        ]

    def stores(what, k):
        return [
            pltpu.make_async_copy(
                result.at[which],
                (layer_out if what == "layer" else tokens_out).at[pl.ds(begin(which, k), size)],
                result_sems.at[which],
            )
            for which in range(2)
        ]

    sequence = [("layer", k) for k in range(4)] + [("tokens", k) for k in range(4)]

    def finish(what, k):
        number = sequence.index((what, k))
        for copy in fetches(what, k):
            copy.wait()
        if number > 0:
            for copy in stores(*sequence[number - 1]):
                copy.wait()
        (outs if what == "layer" else heads).other(k)

        def run(which, row):
            total = stage[0, row, :] if which else own[k, row, :]
            value = wide[which, row, :]
            if what == "layer":
                total = value + total
            else:
                inputs = narrow[which, row, :].astype(jnp.float32)
                inverse = lax.rsqrt(jnp.mean(inputs * inputs, axis=-1, keepdims=True) + epsilon)
                total = value + norm_back(total, inputs, inverse, gain[...])
            result[which, row, :] = total.astype(jnp.bfloat16)

        for which in range(2):
            loop_rows(size, 16, functools.partial(run, which))
        for copy in stores(what, k):
            copy.start()
        if number + 1 < len(sequence):
            for copy in fetches(*sequence[number + 1]):
                copy.start()

    team_send(gate_copies, 1)

    @pl.when(inner == 1)
    def _():
        gate_copies[2].start()

    gains[...] = jnp.zeros_like(gains)
    for copy in fetches("layer", 0):
        copy.start()
    for copy in loads[:2]:
        copy.wait()
    head_send_block(0)
    own_loads[0].wait()
    outs.cores(0)
    for copy in loads[2:]:
        copy.wait()
    up_block(1, up_send.at[0], False)
    y_up[0].start()
    for k in range(1, 4):
        own_loads[k].wait()
        outs.cores(k)
    up_block(2, up_send.at[1], False)
    y_up[1].start()
    for index in range(3, 6):
        head_send_block(index)
    outs.chips(0)
    finish("layer", 0)
    head_take(6)
    line_step(0)
    head_terms(0)
    outs.chips(1)
    finish("layer", 1)
    head_terms(1)
    heads.cores(0)
    y_up[0].wait_recv()
    up_block(7, up_kept.at[0], True)
    team_send(up_copies, 0)
    outs.chips(2)
    finish("layer", 2)
    head_terms(2)
    heads.cores(1)
    outs.chips(3)
    heads.cores(2)
    finish("layer", 3)
    head_terms(3)
    heads.cores(3)
    y_up[1].wait_recv()
    up_block(8, up_kept.at[1], True)
    team_send(up_copies, 1)
    team_forward(up_copies)
    heads.chips(0)
    finish("tokens", 0)
    for k in range(2):
        y_up[k].wait_send()
    team_combine(
        gate_copies, gate_inward, gate_landed.at[0], gate_landed.at[1], gate_ready,
        gate_out, end_sems.at[0], 0,
    )
    head_take(9)
    line_step(1)
    heads.chips(1)
    finish("tokens", 1)
    y_raw[0].wait_send()
    y_head[0].wait_send()
    heads.chips(2)
    finish("tokens", 2)
    head_take(10)
    line_step(2)
    head_block(11, raw_send.at[0], head_send.at[0], False)
    team_combine(
        up_copies, up_landed.at[0], up_landed.at[2], up_landed.at[3], up_kept.at[1],
        up_out, end_sems.at[1], 1,
    )
    heads.chips(3)
    finish("tokens", 3)
    y_raw[high - 1].wait_recv()
    y_head[high - 1].wait_recv()
    for kept, sent, step in ((raw_kept, raw_send, 8), (head_kept, head_send, 16)):

        def run_last(row):
            kept[high - 1, row, :] = kept[high - 1, row, :] + sent[0, row, :]

        loop_rows(kept.shape[1], step, run_last)
    line_end()
    ends = [
        pltpu.make_async_copy(raw_kept.at[high - 1], raw_out, end_sems.at[2]),
        pltpu.make_async_copy(head_kept.at[high - 1], head_out, end_sems.at[3]),
    ]
    for copy in ends:
        copy.start()

    def run_gain(row):
        place_row = pl.ds(pl.multiple_of(own_rows.start + row.start, 16), row.size)
        add_gain(0, row, raw_kept[high - 1, row, :], head_weights[place_row, :])

    loop_rows(width, 16, run_gain)
    own_columns = pl.ds(pl.multiple_of(own_rows.start, 128), width)
    turned = jnp.transpose(gains[...])[:8]
    scale = jnp.concatenate([gain[:, own_columns], feed_gain[:, own_columns]], axis=0)
    gain_rows[:8, :] = turned
    gain_rows[:2, :] = turned[:2] / scale
    gain_rows[8:, :] = raw_kept[high - 1, width:, :width]
    gain_copies = [
        remote(gain_rows, gains_in.at[k], gain_sems, k, device)
        for k, device in enumerate((sibling, facing))
    ]
    for k in range(2):
        gain_copies[k].start()
        gain_copies[k].wait()
        gain_rows[...] = gain_rows[...] + gains_in[k]
    gain_store = pltpu.make_async_copy(gain_rows, gains_out, own_sems.at[0])
    gain_store.start()
    gain_store.wait()
    for k in range(4):
        outs.c_copies[k].wait_send()
        heads.back_copies[k].wait_send()
    for k in range(2, 4):
        heads.c_copies[k].wait_send()
    for k in range(1, high):
        y_raw[k].wait_send()
        y_head[k].wait_send()
    for copy in stores(*sequence[-1]) + ends:
        copy.wait()


def rear(turns, arrays, lines, places, weights, gain, feed_gain):
    rows, depth = places[0].shape
    units = arrays[0].shape[1]
    heads, inner = arrays[8].shape[1], arrays[10].shape[1]
    size = rows // 8
    width = depth // 8
    high = len(turns)
    f32, b16 = jnp.float32, jnp.bfloat16
    any_space = pl.BlockSpec(memory_space=pl.ANY)
    in_vmem = pl.BlockSpec(memory_space=pltpu.VMEM)
    shape = jax.ShapeDtypeStruct
    dma = pltpu.SemaphoreType.DMA
    vmem = pltpu.VMEM
    slots = 2 * (high - 1)
    return pl.pallas_call(
        functools.partial(rear_kernel, size, turns),
        out_shape=[
            shape((rows, depth), b16),
            shape((rows, depth), b16),
            shape((width, units), f32),
            shape((width, units), f32),
            shape((width + 8, heads), f32),
            shape((inner, width), f32),
            shape((16, width), f32),
        ]
        + [shape((4, size, depth), f32)] * 6
        + [shape((2, width, units), f32), shape((4, width, units), f32)],
        in_specs=[any_space] * 11 + [in_vmem] + [any_space] * 9 + [in_vmem] * 2,
        out_specs=[any_space] * 15,
        scratch_shapes=[
            vmem((2 * rows, units), b16),
            vmem((rows, heads), b16),
            vmem((rows, inner), b16),
            vmem((depth, heads), b16),
            vmem((2, width, units), b16),
            vmem((width, HD), f32),
            vmem((16, width), f32),
            vmem((2, 16, width), f32),
            vmem((2, 2 * rows, width), b16),
            vmem((2, width, units), f32),
            vmem((2, width, units), f32),
            vmem((high, width + 8, heads), f32),
            vmem((high, width + 8, heads), f32),
            vmem((high, inner, width), f32),
            vmem((high, inner, width), f32),
            vmem((slots, width + 8, heads), f32),
            vmem((slots, inner, width), f32),
            vmem((4, size, depth), f32),
            vmem((2, size, depth), f32),
            vmem((1, size, depth), f32),
            vmem((2, size, depth), f32),
            vmem((2, size, depth), b16),
            vmem((2, size, depth), b16),
            dma((9,)),
            dma((2, 2)),
            dma((2, 2)),
            dma((2, high)),
            dma((2, high)),
            dma((2, 4)),
            dma((2, 4)),
            dma((2, slots)),
            dma((2, slots)),
            *[dma((2, 4))] * 6,
            dma((4,)),
            dma((1,)),
            dma((2,)),
            dma((2,)),
            dma((2,)),
            dma((6,)),
            dma((2, 2)),
        ],
        compiler_params=pltpu.CompilerParams(
            collective_id=3, has_side_effects=True, vmem_limit_bytes=62 * 1024 * 1024
        ),
        cost_estimate=pl.CostEstimate(
            flops=8 * rows * depth * units, bytes_accessed=6 * depth * units, transcendentals=0
        ),
    )(*arrays, lines, *places, *weights, gain[None], feed_gain[None])


def block_mask(segment_column, segment_row, begin, rows, columns):
    row = begin + lax.broadcasted_iota(jnp.int32, (rows, columns), 0)
    column = lax.broadcasted_iota(jnp.int32, (rows, columns), 1)
    same = segment_column[pl.ds(begin, rows), :] == segment_row[:, :columns]
    return same & (row >= column)


def head_columns(index):
    return pl.ds(pl.multiple_of(index * HD, HD), HD)


def attention_kernel(
    step,
    tokens, gain, query_weight, key_weight, value_weight, query_gain, key_gain, cosine, sine,
    segment_column, segment_row,
    normed_out, query_raw, key_raw, query_out, key_out, value_out, mixed_out, total_out,
):
    count = tokens.shape[0]
    query_heads = query_weight.shape[1] // HD
    value_heads = key_weight.shape[1] // HD
    group = query_heads // value_heads

    def normalize(rows):
        value = tokens[rows, :].astype(jnp.float32)
        normed_out[rows, :] = (value * rms_inverse(value) * gain[...]).astype(jnp.bfloat16)

    loop_rows(count, 32, normalize)

    def project(rows):
        low = normed_out[rows, :]
        value_out[rows, :] = jnp.dot(
            low, value_weight[...], preferred_element_type=jnp.float32
        ).astype(jnp.bfloat16)
        for weight, raw, out, head_gain, heads in (
            (query_weight, query_raw, query_out, query_gain, query_heads),
            (key_weight, key_raw, key_out, key_gain, value_heads),
        ):
            product = jnp.dot(low, weight[...], preferred_element_type=jnp.float32)
            raw[rows, :] = product
            for head in range(heads):
                part = product[:, head * HD : (head + 1) * HD]
                unit = part * rms_inverse(part) * head_gain[...]
                turned = unit * cosine[rows, :] + pltpu.roll(unit, HD // 2, 1) * sine[rows, :]
                out[rows, head * HD : (head + 1) * HD] = turned.astype(jnp.bfloat16)

    loop_rows(count, step, project)

    def head_step(head, carry):
        own = head_columns(head)
        shared = head_columns(head // group)
        for begin in range(0, count, step):
            reach = begin + step
            scores = lax.dot_general(
                query_out[pl.ds(begin, step), own],
                key_out[pl.ds(0, reach), shared],
                (((1,), (1,)), ((), ())),
                preferred_element_type=jnp.float32,
            ) * HD ** (-0.5)
            allowed = block_mask(segment_column, segment_row, begin, step, reach)
            scores = jnp.where(allowed, scores, masked)
            peak = jnp.max(scores, axis=-1, keepdims=True)
            expons = jnp.exp(scores - peak)
            total = jnp.sum(expons, axis=-1, keepdims=True)
            chance = (expons * (1.0 / total)).astype(jnp.bfloat16)
            mixed_out[pl.ds(begin, step), own] = jnp.dot(
                chance, value_out[pl.ds(0, reach), shared], preferred_element_type=jnp.float32
            ).astype(jnp.bfloat16)
            total_out[head, pl.ds(begin, step), :] = jnp.broadcast_to(
                peak + jnp.log(total), (step, HD)
            )
        return carry

    lax.fori_loop(0, query_heads, head_step, 0)


def attention(tokens, gain, weights, query_gain, key_gain, cosine, sine, segment_column, segment_row):
    count, depth = tokens.shape
    queries, keys = weights[0].shape[1], weights[1].shape[1]
    f32, b16 = jnp.float32, jnp.bfloat16
    shape = jax.ShapeDtypeStruct
    return pl.pallas_call(
        functools.partial(attention_kernel, 256),
        out_shape=[
            shape((count, depth), b16),
            shape((count, queries), f32),
            shape((count, keys), f32),
            shape((count, queries), b16),
            shape((count, keys), b16),
            shape((count, keys), b16),
            shape((count, queries), b16),
            shape((queries // HD, count, HD), f32),
        ],
        compiler_params=pltpu.CompilerParams(vmem_limit_bytes=56 * 1024 * 1024),
        cost_estimate=pl.CostEstimate(
            flops=2 * count * depth * (queries + 2 * keys) + 4 * count * count * queries,
            bytes_accessed=32 * 1024 * 1024,
            transcendentals=count * count * queries // HD,
        ),
    )(tokens, gain[None], *weights, query_gain[None], key_gain[None], cosine, sine, segment_column, segment_row)


def attention_back_kernel(
    step,
    hidden_low, output_weight, queries, keys, values, totals, query_raw, key_raw,
    query_gain, key_gain, cosine, sine, segment_column, segment_row,
    raw_out, query_gain_out, key_gain_out,
    upstream, query_grad, key_grad, value_grad,
):
    count = hidden_low.shape[0]
    query_heads = queries.shape[1] // HD
    value_heads = keys.shape[1] // HD
    group = query_heads // value_heads
    across_last = (((1,), (1,)), ((), ()))
    down_first = (((0,), (0,)), ((), ()))

    def project(rows):
        upstream[rows, :] = lax.dot_general(
            hidden_low[rows, :],
            output_weight[...],
            across_last,
            preferred_element_type=jnp.float32,
        ).astype(jnp.bfloat16)

    loop_rows(count, step, project)
    key_grad[...] = jnp.zeros_like(key_grad)
    value_grad[...] = jnp.zeros_like(value_grad)

    def head_step(head, carry):
        own = head_columns(head)
        shared = head_columns(head // group)
        for begin in range(0, count, step):
            reach = begin + step
            rows, before = pl.ds(begin, step), pl.ds(0, reach)
            scores = lax.dot_general(
                queries[rows, own],
                keys[before, shared],
                across_last,
                preferred_element_type=jnp.float32,
            ) * HD ** (-0.5)
            allowed = block_mask(segment_column, segment_row, begin, step, reach)
            chance = jnp.exp(jnp.where(allowed, scores, masked) - totals[head, rows, :][:, :1])
            incoming = upstream[rows, own]
            value_grad[before, shared] += lax.dot_general(
                chance.astype(jnp.bfloat16),
                incoming,
                down_first,
                preferred_element_type=jnp.float32,
            )
            along = lax.dot_general(
                incoming, values[before, shared], across_last, preferred_element_type=jnp.float32
            )
            center = jnp.sum(along * chance, axis=-1, keepdims=True)
            score_grad = (chance * (along - center)).astype(jnp.bfloat16)
            query_grad[rows, own] = jnp.dot(
                score_grad, keys[before, shared], preferred_element_type=jnp.float32
            ) * HD ** (-0.5)
            key_grad[before, shared] += lax.dot_general(
                score_grad, queries[rows, own], down_first, preferred_element_type=jnp.float32
            ) * HD ** (-0.5)
        return carry

    lax.fori_loop(0, query_heads, head_step, 0)
    query_gain_out[...] = jnp.zeros_like(query_gain_out)
    key_gain_out[...] = jnp.zeros_like(key_gain_out)

    def finish(rows):
        for grad, raw, head_gain, gain_out, heads, place in (
            (query_grad, query_raw, query_gain, query_gain_out, query_heads, 0),
            (key_grad, key_raw, key_gain, key_gain_out, value_heads, query_heads),
        ):
            for head in range(heads):
                columns = slice(head * HD, (head + 1) * HD)
                upward = grad[rows, columns]
                unit_grad = upward * cosine[rows, :] - pltpu.roll(upward, HD // 2, 1) * sine[rows, :]
                value = raw[rows, columns]
                inverse = rms_inverse(value)
                product = unit_grad * (value * inverse)
                gain_out[...] += jnp.sum(product.reshape(-1, 8, HD), axis=0)
                begin = (place + head) * HD
                raw_out[rows, begin : begin + HD] = norm_back(
                    unit_grad, value, inverse, head_gain[...]
                ).astype(jnp.bfloat16)
        begin = (query_heads + value_heads) * HD
        raw_out[rows, begin:] = value_grad[rows, :].astype(jnp.bfloat16)

    loop_rows(count, 64, finish)


def attention_back(
    hidden_low, output_weight, queries, keys, values, totals, query_raw, key_raw,
    query_gain, key_gain, cosine, sine, segment_column, segment_row,
):
    count = hidden_low.shape[0]
    query_columns, key_columns = queries.shape[1], keys.shape[1]
    f32, b16 = jnp.float32, jnp.bfloat16
    shape = jax.ShapeDtypeStruct
    return pl.pallas_call(
        functools.partial(attention_back_kernel, 256),
        out_shape=[
            shape((count, query_columns + 2 * key_columns), b16),
            shape((8, HD), f32),
            shape((8, HD), f32),
        ],
        scratch_shapes=[
            pltpu.VMEM((count, query_columns), b16),
            pltpu.VMEM((count, query_columns), f32),
            pltpu.VMEM((count, key_columns), f32),
            pltpu.VMEM((count, key_columns), f32),
        ],
        compiler_params=pltpu.CompilerParams(vmem_limit_bytes=56 * 1024 * 1024),
        cost_estimate=pl.CostEstimate(
            flops=2 * count * hidden_low.shape[1] * query_columns + 10 * count * count * query_columns,
            bytes_accessed=24 * 1024 * 1024,
            transcendentals=count * count * query_columns // HD,
        ),
    )(
        hidden_low, output_weight, queries, keys, values, totals, query_raw, key_raw,
        query_gain[None], key_gain[None], cosine, sine, segment_column, segment_row,
    )


def finish_kernel(columns, number, *refs):
    inputs, gains = refs[:number], refs[number]
    outs, held = refs[number + 1 : -number - 2], refs[-number - 2 : -2]
    in_sems, out_sems = refs[-2:]
    rows = outs[number - 1].shape[0]
    fetches = [
        pltpu.make_async_copy(source, target, in_sems.at[index])
        for index, (source, target) in enumerate(zip(inputs, held))
    ]
    for copy in fetches:
        copy.start()
    stores = [[pltpu.make_async_copy(held[k], outs[k], out_sems.at[k])] for k in range(number - 1)]
    begin, last = 0, []
    for k, count in enumerate(columns):
        last.append(
            pltpu.make_async_copy(
                held[-1].at[pl.ds(0, rows), pl.ds(begin, count)],
                outs[number - 1 + k],
                out_sems.at[number - 1 + k],
            )
        )
        begin += count
    stores.append(last)
    for row, out in zip((0, 1, 8, 9), outs[number + 2 :]):
        out[...] = gains[row : row + 1, : out.shape[1]]
    for fetch, group in zip(fetches, stores):
        fetch.wait()
        for copy in group:
            copy.start()
    for group in stores:
        for copy in group:
            copy.wait()


def finish(columns, head_width, arrays, raw, gains):
    shape = jax.ShapeDtypeStruct
    any_space = pl.BlockSpec(memory_space=pl.ANY)
    in_vmem = pl.BlockSpec(memory_space=pltpu.VMEM)
    width = raw.shape[0] - 8
    number = len(arrays) + 1
    outs = [shape(value.shape, value.dtype) for value in arrays]
    outs += [shape((width, count), jnp.float32) for count in columns]
    outs += [shape((1, count), jnp.float32) for count in (width, width, head_width, head_width)]
    return pl.pallas_call(
        functools.partial(finish_kernel, columns, number),
        out_shape=outs,
        in_specs=[any_space] * number + [in_vmem],
        out_specs=[any_space] * (number + 2) + [in_vmem] * 4,
        scratch_shapes=[pltpu.VMEM(value.shape, value.dtype) for value in (*arrays, raw)]
        + [pltpu.SemaphoreType.DMA((number,)), pltpu.SemaphoreType.DMA((number + 2,))],
        compiler_params=pltpu.CompilerParams(vmem_limit_bytes=60 * 1024 * 1024),
    )(*arrays, raw, gains)


def plain_shards(
    tokens,
    attention_gain,
    query_weight,
    key_weight,
    value_weight,
    query_gain,
    key_gain,
    output_weight,
    feedforward_gain,
    gate_weight,
    up_weight,
    down_weight,
    segment_numbers,
    positions,
    cotangent,
):
    count = tokens.shape[0]
    batch = count // SEQ_LEN
    query_heads = query_weight.shape[1] // HD
    value_heads = key_weight.shape[1] // HD
    group = query_heads // value_heads
    inputs = tokens.astype(jnp.float32)
    first_inverse = rms_inverse(inputs)
    first_normed = inputs * first_inverse
    normed_low = (first_normed * attention_gain).astype(jnp.bfloat16)
    query_raw = jnp.dot(normed_low, query_weight, preferred_element_type=jnp.float32).reshape(
        count, query_heads, HD
    )
    key_raw = jnp.dot(normed_low, key_weight, preferred_element_type=jnp.float32).reshape(
        count, value_heads, HD
    )
    value_low = jnp.dot(normed_low, value_weight, preferred_element_type=jnp.float32).astype(
        jnp.bfloat16
    )
    cosine, sine = rotary_tables(positions)
    cosine = cosine[:, None]
    sine = sine[:, None]
    query_inverse = rms_inverse(query_raw)
    query_unit = query_raw * query_inverse
    query_low = rotate(query_unit * query_gain, cosine, sine).astype(jnp.bfloat16)
    key_inverse = rms_inverse(key_raw)
    key_unit = key_raw * key_inverse
    key_low = rotate(key_unit * key_gain, cosine, sine).astype(jnp.bfloat16)
    queries = query_low.reshape(batch, SEQ_LEN, value_heads, group, HD)
    keys = key_low.reshape(batch, SEQ_LEN, value_heads, HD)
    values = value_low.reshape(batch, SEQ_LEN, value_heads, HD)
    segments = segment_numbers.reshape(batch, SEQ_LEN)
    mixed, totals = lax.map(attend, (queries, keys, values, segments))
    mixed_low = mixed.reshape(count, query_heads * HD).astype(jnp.bfloat16)
    attention = lax.psum(
        jnp.dot(mixed_low, output_weight, preferred_element_type=jnp.float32), "tensor"
    )
    hidden = inputs + attention
    second_inverse = rms_inverse(hidden)
    second_normed = hidden * second_inverse
    second_low = (second_normed * feedforward_gain).astype(jnp.bfloat16)
    gate = jnp.dot(second_low, gate_weight, preferred_element_type=jnp.float32)
    upward = jnp.dot(second_low, up_weight, preferred_element_type=jnp.float32)
    sigmoid_gate = jax.nn.sigmoid(gate)
    activated = gate * sigmoid_gate
    product_low = (activated * upward).astype(jnp.bfloat16)
    feedforward = lax.psum(
        jnp.dot(product_low, down_weight, preferred_element_type=jnp.float32), "tensor"
    )
    layer_output = (hidden + feedforward).astype(jnp.bfloat16)
    down_grad = jnp.einsum("tf,td->fd", product_low, cotangent, preferred_element_type=jnp.float32)
    product_grad = jnp.einsum(
        "td,fd->tf", cotangent, down_weight, preferred_element_type=jnp.float32
    )
    gate_grad_low = (
        product_grad * upward * sigmoid_gate * (1.0 + gate * (1.0 - sigmoid_gate))
    ).astype(jnp.bfloat16)
    upward_grad_low = (product_grad * activated).astype(jnp.bfloat16)
    gate_weight_grad = jnp.einsum(
        "td,tf->df", second_low, gate_grad_low, preferred_element_type=jnp.float32
    )
    upward_weight_grad = jnp.einsum(
        "td,tf->df", second_low, upward_grad_low, preferred_element_type=jnp.float32
    )
    second_part = jnp.einsum(
        "tf,df->td", gate_grad_low, gate_weight, preferred_element_type=jnp.float32
    )
    second_part = second_part + jnp.einsum(
        "tf,df->td", upward_grad_low, up_weight, preferred_element_type=jnp.float32
    )
    second_grad = lax.psum(second_part, "tensor")
    second_gain_grad = jnp.sum(second_grad * second_normed, axis=0)
    hidden_grad = cotangent.astype(jnp.float32) + norm_back(
        second_grad, hidden, second_inverse, feedforward_gain
    )
    hidden_low = hidden_grad.astype(jnp.bfloat16)
    output_weight_grad = jnp.einsum(
        "tc,td->cd", mixed_low, hidden_low, preferred_element_type=jnp.float32
    )
    mixed_grad = jnp.einsum(
        "td,cd->tc", hidden_low, output_weight, preferred_element_type=jnp.float32
    ).astype(jnp.bfloat16)
    upstream = mixed_grad.reshape(batch, SEQ_LEN, value_heads, group, HD)
    query_back, key_back, value_back = lax.map(
        attend_back, (queries, keys, values, segments, totals, upstream)
    )
    query_unit_grad = rotate_back(query_back.reshape(count, query_heads, HD), cosine, sine)
    key_unit_grad = rotate_back(key_back.reshape(count, value_heads, HD), cosine, sine)
    query_gain_part = jnp.sum(query_unit_grad * query_unit, axis=(0, 1))
    key_gain_part = jnp.sum(key_unit_grad * key_unit, axis=(0, 1))
    query_raw_grad = (
        norm_back(query_unit_grad, query_raw, query_inverse, query_gain)
        .reshape(count, query_heads * HD)
        .astype(jnp.bfloat16)
    )
    key_raw_grad = (
        norm_back(key_unit_grad, key_raw, key_inverse, key_gain)
        .reshape(count, value_heads * HD)
        .astype(jnp.bfloat16)
    )
    value_raw_grad = value_back.reshape(count, value_heads * HD).astype(jnp.bfloat16)
    query_weight_grad = jnp.einsum(
        "td,tc->dc", normed_low, query_raw_grad, preferred_element_type=jnp.float32
    )
    key_weight_grad = jnp.einsum(
        "td,tc->dc", normed_low, key_raw_grad, preferred_element_type=jnp.float32
    )
    value_weight_grad = jnp.einsum(
        "td,tc->dc", normed_low, value_raw_grad, preferred_element_type=jnp.float32
    )
    first_part = jnp.einsum(
        "tc,dc->td", query_raw_grad, query_weight, preferred_element_type=jnp.float32
    )
    first_part = first_part + jnp.einsum(
        "tc,dc->td", key_raw_grad, key_weight, preferred_element_type=jnp.float32
    )
    first_part = first_part + jnp.einsum(
        "tc,dc->td", value_raw_grad, value_weight, preferred_element_type=jnp.float32
    )
    first_grad, query_gain_grad, key_gain_grad = lax.psum(
        (first_part, query_gain_part, key_gain_part), "tensor"
    )
    first_gain_grad = jnp.sum(first_grad * first_normed, axis=0)
    tokens_gradient = (
        hidden_grad + norm_back(first_grad, inputs, first_inverse, attention_gain)
    ).astype(jnp.bfloat16)
    summed = (
        lax.psum_scatter(first_gain_grad, "dp", scatter_dimension=0, tiled=True),
        lax.psum_scatter(query_weight_grad, "dp", scatter_dimension=0, tiled=True),
        lax.psum_scatter(key_weight_grad, "dp", scatter_dimension=0, tiled=True),
        lax.psum_scatter(value_weight_grad, "dp", scatter_dimension=0, tiled=True),
        lax.psum_scatter(query_gain_grad, "dp", scatter_dimension=0, tiled=True),
        lax.psum_scatter(key_gain_grad, "dp", scatter_dimension=0, tiled=True),
        lax.psum_scatter(output_weight_grad, "dp", scatter_dimension=1, tiled=True),
        lax.psum_scatter(second_gain_grad, "dp", scatter_dimension=0, tiled=True),
        lax.psum_scatter(gate_weight_grad, "dp", scatter_dimension=0, tiled=True),
        lax.psum_scatter(upward_weight_grad, "dp", scatter_dimension=0, tiled=True),
        lax.psum_scatter(down_grad, "dp", scatter_dimension=1, tiled=True),
    )
    return (
        layer_output,
        tokens_gradient,
        summed[0],
        summed[1],
        summed[2],
        summed[3],
        summed[4],
        summed[5],
        summed[6],
        summed[7],
        summed[8],
        summed[9],
        summed[10],
    )


def shards(
    dp,
    tokens,
    attention_gain,
    query_weight,
    key_weight,
    value_weight,
    query_gain,
    key_gain,
    output_weight,
    feedforward_gain,
    gate_weight,
    up_weight,
    down_weight,
    segment_numbers,
    positions,
    cotangent,
):
    count, depth = tokens.shape
    width = depth // dp
    high = dp // 2
    core = lax.axis_index("tensor") % 2
    upstream_first = lax.ppermute(
        lax.dynamic_slice_in_dim(cotangent, core * (count // 2), 3 * count // 16, 0).astype(jnp.float32),
        "dp",
        [(i, i ^ 2) for i in range(dp)],
    )

    cosine, sine = rotary_tables(positions)
    sine = jnp.concatenate([-sine[:, : HD // 2], sine[:, HD // 2 :]], axis=1)
    tables = (cosine, sine, segment_numbers[:, None], segment_numbers[None])
    normed_low, query_raw, key_raw, queries, keys, values, mixed_low, totals = attention(
        tokens,
        attention_gain,
        (query_weight, key_weight, value_weight),
        query_gain,
        key_gain,
        *tables,
    )
    (
        hidden,
        second_part,
        low_own,
        product_own,
        gate_own,
        upward_own,
        low_pair,
        product_pair,
        gate_pair,
        upward_pair,
        upstream_pair,
    ) = front(
        mixed_low,
        output_weight,
        tokens,
        cotangent,
        upstream_first,
        feedforward_gain,
        gate_weight,
        up_weight,
        down_weight,
    )[:11]
    hidden_grad, hidden_low, out_part, down_weight_grad, gate_ready, gate_given, gate_kept = middle(
        second_part,
        hidden,
        cotangent,
        upstream_pair,
        product_own,
        product_pair,
        gate_own,
        gate_pair,
        low_own,
        low_pair,
        feedforward_gain,
        down_weight,
    )
    gate_middle, gate_inward = (
        lax.ppermute(gate_ready, "dp", [(2 * a + k, 2 * b + k) for a, b in pairs for k in (0, 1)])
        for pairs in (((1, 2), (2, 1)), ((0, 1), (3, 2)))
    )
    gate_moved = lax.ppermute(gate_given, "dp", [(i, i ^ 1) for i in range(dp)])
    raw_grad, query_gain_part, key_gain_part = attention_back(
        hidden_low,
        output_weight,
        queries,
        keys,
        values,
        totals,
        query_raw,
        key_raw,
        query_gain,
        key_gain,
        *tables,
    )

    lines = [
        jnp.pad(value.reshape(dp, -1), ((0, 0), (0, raw_grad.shape[1] - value.size // dp)))
        for value in (jnp.sum(query_gain_part, axis=0), jnp.sum(key_gain_part, axis=0))
    ]
    gain_lines = jnp.pad(jnp.stack(lines, axis=1), ((0, 0), (0, 6), (0, 0)))

    (
        layer_output,
        tokens_gradient,
        gate_weight_grad,
        up_weight_grad,
        raw_whole,
        output_weight_grad,
        gains,
    ) = (
        rear(
            [line_order(high, p) for p in range(high)],
            [gate_middle, gate_inward, gate_kept + gate_moved]
            + [low_own, low_pair, upward_own, upward_pair]
            + [normed_low, raw_grad, hidden_low, mixed_low],
            gain_lines,
            [out_part, hidden, hidden_grad, tokens],
            [query_weight, key_weight, value_weight, gate_weight, up_weight],
            attention_gain,
            feedforward_gain,
        )[:7]
    )
    (
        layer_output,
        tokens_gradient,
        gate_weight_grad,
        up_weight_grad,
        output_weight_grad,
        down_weight_grad,
        query_weight_grad,
        key_weight_grad,
        value_weight_grad,
        attention_gain_grad,
        feedforward_gain_grad,
        query_gain_grad,
        key_gain_grad,
    ) = finish(
        (query_weight.shape[1], key_weight.shape[1], value_weight.shape[1]),
        HD // dp,
        [
            layer_output,
            tokens_gradient,
            gate_weight_grad,
            up_weight_grad,
            output_weight_grad,
            down_weight_grad,
        ],
        raw_whole,
        gains,
    )
    return (
        layer_output,
        tokens_gradient,
        attention_gain_grad[0],
        query_weight_grad,
        key_weight_grad,
        value_weight_grad,
        query_gain_grad[0],
        key_gain_grad[0],
        output_weight_grad,
        feedforward_gain_grad[0],
        gate_weight_grad,
        up_weight_grad,
        down_weight_grad,
    )


def solution(mesh):
    dp, tensor = mesh.shape["dp"], mesh.shape["tensor"]

    def program(*args):
        if dp == 8 and tensor == 4 and args[0].shape[0] == SEQ_LEN:
            return shards(dp, *args)
        return plain_shards(*args)

    return jax.shard_map(
        program,
        mesh=mesh,
        in_specs=(
            P("dp", None),
            P(),
            P(None, "tensor"),
            P(None, "tensor"),
            P(None, "tensor"),
            P(),
            P(),
            P("tensor", None),
            P(),
            P(None, "tensor"),
            P(None, "tensor"),
            P("tensor", None),
            P("dp"),
            P("dp"),
            P("dp", None),
        ),
        out_specs=(
            P("dp", None),
            P("dp", None),
            P("dp"),
            P("dp", "tensor"),
            P("dp", "tensor"),
            P("dp", "tensor"),
            P("dp"),
            P("dp"),
            P("tensor", "dp"),
            P("dp"),
            P("dp", "tensor"),
            P("dp", "tensor"),
            P("tensor", "dp"),
        ),
        check_vma=False,
    )
```

profile of v0, /device:TPU:24, one launch (start us, length us, event | category | flops | bytes accessed | tf_op | source)
XLA Modules:
  0.0 615.3 jit_solution(9027867211470167596)
XLA Ops:
  0.7 1.3 dynamic-slice_convert_fusion
  2.0 0.5 collective-permute-start
  2.5 0.7 convert_element_type.11
  3.2 1.7 copy.28.segment_column
  4.9 0.2 broadcast_multiply_fusion
  5.1 2.7 fusion
  7.8 0.2 slice_negate_fusion
  8.0 1.0 pad_maximum_fusion.1.sine
  9.0 25.9 %shard_map.246 = (bf16[1024,2048]{1,0:T(8,128)(2,1)}, f32[1024,512]{1,0:T(8,128)}, f32[1024,256]{1,0:T(8,128)}, bf16[1024,512]{1,0:T(8,128)(2,1)}, bf16[1024,256...) custom-call(bf16[1024,2048]{1,0:T(8,128)(2,1)} %tokens_hbm.3, ...), custom_call_target="tpu_custom_call" | custom-call | flops 6442450944 | bytes 33554432 | tf_op jit(solution)/shard_map/pallas_call | solution.py:1681
  34.9 3.2 collective-permute-done.upstream_first
  38.2 1.1 copy-done.1
  39.3 168.4 %shard_map.247 = (f32[1024,2048]{1,0:T(8,128)}, f32[1024,2048]{1,0:T(8,128)}, bf16[1024,2048]{1,0:T(8,128)(2,1)}, bf16[1024,1536]{1,0:T(8,128)(2,1)}, bf16[1024,...) custom-call(bf16[1024,512]{1,0:T(8,128)(2,1)} %get-tuple-element.62., ...), custom_call_target="tpu_custom_call" | custom-call | flops 38654705664 | bytes 18874368 | tf_op jit(solution)/shard_map/pallas_call | solution.py:582
  207.7 113.8 %shard_map.248 = (f32[1024,2048]{1,0:T(8,128)}, bf16[1024,2048]{1,0:T(8,128)(2,1)}, f32[1024,2048]{1,0:T(8,128)}, f32[1536,256]{1,0:T(8,128)}, f32[256,1536]{1,0...) custom-call(f32[1024,2048]{1,0:T(8,128)} %get-tuple-element.63.second_hbm, ...), custom_call_target="tpu_custom_call" | custom-call | flops 25769803776 | bytes 18874368 | tf_op jit(solution)/shard_map/pallas_call | solution.py:958
  321.5 1.6 collective-permute-start.3
  323.1 4.9 collective-permute-start.2
  328.0 1.8 collective-permute-start.1
  329.9 29.6 %shard_map.249 = (bf16[1024,1024]{1,0:T(8,128)(2,1)}, f32[8,128]{1,0:T(8,128)}, f32[8,128]{1,0:T(8,128)}) custom-call(bf16[1024,2048]{1,0:T(8,128)(2,1)} %get-tuple-element.78.hidden_low.hidden_low_hbm, bf16[512,2048]{1,0:T(8,128)(2,1)} %output_weight.1, bf16[1024,512]{1,0:T(8,128)(2,1)} %get-tuple-element.79.queries, ...), custom_call_target="tpu_custom_call" | custom-call | flops 7516192768 | bytes 25165824 | tf_op jit(solution)/shard_map/pallas_call | solution.py:1797
  359.4 0.7 reduce_sum.18
  360.1 0.7 reduce_sum.19
  360.8 0.1 reshape.40
  361.1 0.8 select_maximum_fusion.lines
  361.9 1.3 add.18.gate_ready
  363.2 239.9 %shard_map.250 = (bf16[1024,2048]{1,0:T(8,128)(2,1)}, bf16[1024,2048]{1,0:T(8,128)(2,1)}, f32[256,1536]{1,0:T(8,128)}, f32[256,1536]{1,0:T(8,128)}, f32[264,1024...) custom-call(f32[256,1536]{1,0:T(8,128)} %collective-permute-done.1.g, ...), custom_call_target="tpu_custom_call" | custom-call | flops 25769803776 | bytes 18874368 | tf_op jit(solution)/shard_map/pallas_call | solution.py:1535
  603.1 11.9 %shard_map.251 = (bf16[1024,2048]{1,0:T(8,128)(2,1)}, bf16[1024,2048]{1,0:T(8,128)(2,1)}, f32[256,1536]{1,0:T(8,128)}, f32[256,1536]{1,0:T(8,128)}, f32[512,256]...) custom-call(bf16[1024,2048]{1,0:T(8,128)(2,1)} %get-tuple-element.90, ...), custom_call_target="tpu_custom_call" | custom-call | tf_op jit(solution)/shard_map/pallas_call | solution.py:1865
  (12 shorter events, 0.2 us)
Async XLA Ops:
  2.0 36.2 %collective-permute-start = (f32[192,2048]{1,0:T(8,128)S(1)}, f32[192,2048]{1,0:T(8,128)S(1)}, u32[]{:S(2)}, u32[]{:S(2)}) collective-permute-start(f32[192,2048]{1,0:T(8,128)S(1)} %dynamic-slice_convert_fusion), channel_id=1, source_target_pairs={{0,8},{4,12},{8,0},{12,4},{16,24},{20,28},{24,16},{28,20},{1,9},{5... | collective-permute-start | bytes 4718600 | tf_op jit(solution)/shard_map/ppermute | solution.py:2070
  38.2 1.1 copy-start.1
  321.5 40.4 %collective-permute-start.3 = (f32[256,1536]{1,0:T(8,128)}, f32[256,1536]{1,0:T(8,128)S(1)}, u32[]{:S(2)}, u32[]{:S(2)}) collective-permute-start(f32[256,1536]{1,0:T(8,128)} %get-tuple-element.74), channel_id=1, source_target_pairs={{0,4},{4,0},{8,12},{12,8},{16,20},{20,16},{24,28},{28,24},{1,5},{5... | collective-permute-start | bytes 4718600 | tf_op jit(solution)/shard_map/ppermute | solution.py:2128
  323.1 40.1 %collective-permute-start.2 = (f32[256,1536]{1,0:T(8,128)}, f32[256,1536]{1,0:T(8,128)}, u32[]{:S(2)}, u32[]{:S(2)}) collective-permute-start(f32[256,1536]{1,0:T(8,128)} %get-tuple-element.72), channel_id=1, source_target_pairs={{0,8},{4,12},{24,16},{28,20},{1,9},{5,13},{25,17},{29,21},{2,10},{... | collective-permute-start | bytes 4718600 | tf_op jit(solution)/shard_map/ppermute | solution.py:2125
  328.0 35.2 %collective-permute-start.1 = (f32[256,1536]{1,0:T(8,128)}, f32[256,1536]{1,0:T(8,128)}, u32[]{:S(2)}, u32[]{:S(2)}) collective-permute-start(f32[256,1536]{1,0:T(8,128)} %get-tuple-element.72), channel_id=1, source_target_pairs={{8,16},{12,20},{16,8},{20,12},{9,17},{13,21},{17,9},{21,13},{10,18... | collective-permute-start | bytes 4718600 | tf_op jit(solution)/shard_map/ppermute | solution.py:2125
  329.9 32.0 %copy-start = (f32[256,1536]{1,0:T(8,128)S(1)}, f32[256,1536]{1,0:T(8,128)}, u32[]{:S(2)}) copy-start(f32[256,1536]{1,0:T(8,128)} %get-tuple-element.73) | copy-start | bytes 4718596
where the time goes:
time: 625 us; the launch traced here: 615 us
  Pallas kernels  590 us (94%)
  other arithmetic  9.64 us (2%)
  starting transfers between devices  8.87 us (1%)
    pallas_call x1, Pallas kernels, rear(): pl.pallas_call(functools.partial(rear_kernel, size, turns), out_shape=[sh...  240 us
    pallas_call x1, Pallas kernels, front(): pl.pallas_call(functools.partial(front_kernel, size, first), out_shape=ou...  168 us
    pallas_call x1, Pallas kernels, middle(): pl.pallas_call(functools.partial(middle_kernel, size), out_shape=[shape((...  114 us
    pallas_call x1, Pallas kernels, attention_back(): pl.pallas_call(functools.partial(attention_back_kernel, 256), out_shape=[...  29.6 us
    pallas_call x1, Pallas kernels, attention(): pl.pallas_call(functools.partial(attention_kernel, 256), out_shape=[shape...  25.9 us
  transfers between devices with their start and end apart: 4, of which 1 were waited for; matrix products, arithmetic and copies ran while one was open for 2% of the time, Pallas kernels for 9%

commit v1 on v0

--- a/solution.py
+++ b/solution.py
@@ -433,7 +433,7 @@
             for copy in wave_copies(tiles.at[which], outs[which], tile_sems.at[which], wave)
         ]
 
-    feeds = [(0, 0), (0, 1), (1, 0), (1, 1)]
+    feeds = [(0, 0), (1, 0), (0, 1), (1, 1)]
 
     def fetches(wave):
         return wave_copies(rows16, upstream_hbm, wave_sems.at[0], wave, True)
@@ -445,7 +445,7 @@
             if number > 0:
                 for copy in tile_stores(*feeds[number - 1]):
                     copy.wait()
-        if index == 0:
+        if index == 0 and not part:
             for copy in fetches(wave):
                 copy.wait()
 
@@ -476,26 +476,27 @@
             if part is None or number % 4 // 2 == part:
                 copy.start()
         if index == 0:
-            if wave > 0:
+            if wave > 0 and not part:
                 for copy in term_stores(wave - 1):
                     copy.wait()
 
             def second(column):
-                terms[:, column] = lax.dot_general(
-                    tiles[1],
+                terms[rows, column] = lax.dot_general(
+                    tiles[1, rows],
                     gate_weight[column, :],
                     across_last,
                     preferred_element_type=jnp.float32,
                 ) + lax.dot_general(
-                    tiles[2],
+                    tiles[2, rows],
                     up_weight[column, :],
                     across_last,
                     preferred_element_type=jnp.float32,
                 )
 
-            loop_rows(depth, 512, second)
-            for copy in term_stores(wave):
-                copy.start()
+            loop_rows(depth, 1024 if part is not None else 512, second)
+            for number, copy in enumerate(term_stores(wave)):
+                if part is None or number // 2 == part:
+                    copy.start()
 
     for load in token_loads(0):
         load.start()
@@ -522,29 +523,31 @@
     normed(0)
     for load in loads[3:]:
         load.wait()
+    for k in range(4):
+        c_copies[k].wait_send()
+    feed(0, 0, 0)
     attention_chips(1)
     normed(1)
     upstream_forward(2)
-    for k in range(4):
-        c_copies[k].wait_send()
-    feed(0, 0)
+    feed(0, 0, 1)
     attention_chips(2)
     for copy in low_stores(0, 0):
         copy.wait()
     normed(2)
     pair_forward(0)
-    upstream_wave(0)
+    for copy in fetches(1):
+        copy.start()
+    feed(1, 0, 0)
     attention_chips(3)
     normed(3)
+    feed(1, 0, 1)
     pair_forward(1)
+    upstream_wave(0)
     pair_rows((0, 1))
     feed(0, 1)
     for copy in pair_stores(0):
         copy.wait()
-    for copy in fetches(1):
-        copy.start()
     pair_forward(2)
-    feed(1, 0)
     upstream_wave(1)
     for copy in low_stores(0, 1):
         copy.wait()

time: 625 us -> 617 us (0.987)
  Pallas kernels: 590 us -> 580 us
    pallas_call x1, Pallas kernels: 168 us -> 159 us  [front(): pl.pallas_call(functools.partial(front_kernel, size, first), out_shape=ou...]
where the time goes in v1:
time: 617 us; the launch traced here: 607 us
  Pallas kernels  580 us (94%)
  starting transfers between devices  10.2 us (2%)
  other arithmetic  9.64 us (2%)
    pallas_call x1, Pallas kernels, rear(): pl.pallas_call(functools.partial(rear_kernel, size, turns), out_shape=[sh...  240 us
    pallas_call x1, Pallas kernels, front(): pl.pallas_call(functools.partial(front_kernel, size, first), out_shape=ou...  159 us
    pallas_call x1, Pallas kernels, middle(): pl.pallas_call(functools.partial(middle_kernel, size), out_shape=[shape((...  114 us
    pallas_call x1, Pallas kernels, attention_back(): pl.pallas_call(functools.partial(attention_back_kernel, 256), out_shape=[...  29.6 us
    pallas_call x1, Pallas kernels, attention(): pl.pallas_call(functools.partial(attention_kernel, 256), out_shape=[shape...  25.9 us
  transfers between devices with their start and end apart: 4, of which 1 were waited for; matrix products, arithmetic and copies ran while one was open for 2% of the time, Pallas kernels for 9%

profile of v1, /device:TPU:24, one launch (start us, length us, event | category | flops | bytes accessed | tf_op | source)
XLA Modules:
  0.0 607.2 jit_solution(10253579128552904309)
XLA Ops:
  0.7 1.3 dynamic-slice_convert_fusion
  2.0 0.5 collective-permute-start
  2.5 0.7 convert_element_type.11
  3.2 1.7 copy.28.segment_column
  4.9 0.2 broadcast_multiply_fusion
  5.1 2.7 fusion
  7.8 0.2 slice_negate_fusion
  8.0 1.0 pad_maximum_fusion.1.sine
  9.0 25.9 %shard_map.246 = (bf16[1024,2048]{1,0:T(8,128)(2,1)}, f32[1024,512]{1,0:T(8,128)}, f32[1024,256]{1,0:T(8,128)}, bf16[1024,512]{1,0:T(8,128)(2,1)}, bf16[1024,256...) custom-call(bf16[1024,2048]{1,0:T(8,128)(2,1)} %tokens_hbm.3, ...), custom_call_target="tpu_custom_call" | custom-call | flops 6442450944 | bytes 33554432 | tf_op jit(solution)/shard_map/pallas_call | solution.py:1684
  34.9 3.2 collective-permute-done.upstream_first
  38.2 1.1 copy-done.1
  39.3 159.0 %shard_map.247 = (f32[1024,2048]{1,0:T(8,128)}, f32[1024,2048]{1,0:T(8,128)}, bf16[1024,2048]{1,0:T(8,128)(2,1)}, bf16[1024,1536]{1,0:T(8,128)(2,1)}, bf16[1024,...) custom-call(bf16[1024,512]{1,0:T(8,128)(2,1)} %get-tuple-element.62., ...), custom_call_target="tpu_custom_call" | custom-call | flops 38654705664 | bytes 18874368 | tf_op jit(solution)/shard_map/pallas_call | solution.py:585
  198.3 113.6 %shard_map.248 = (f32[1024,2048]{1,0:T(8,128)}, bf16[1024,2048]{1,0:T(8,128)(2,1)}, f32[1024,2048]{1,0:T(8,128)}, f32[1536,256]{1,0:T(8,128)}, f32[256,1536]{1,0...) custom-call(f32[1024,2048]{1,0:T(8,128)} %get-tuple-element.63.second_hbm, ...), custom_call_target="tpu_custom_call" | custom-call | flops 25769803776 | bytes 18874368 | tf_op jit(solution)/shard_map/pallas_call | solution.py:961
  311.9 1.6 collective-permute-start.3
  313.5 6.3 %collective-permute-start.2 = (f32[256,1536]{1,0:T(8,128)}, f32[256,1536]{1,0:T(8,128)}, u32[]{:S(2)}, u32[]{:S(2)}) collective-permute-start(f32[256,1536]{1,0:T(8,128)} %get-tuple-element.72), channel_id=1, source_target_pairs={{0,8},{4,12},{24,16},{28,20},{1,9},{5,13},{25,17},{29,21},{2,10},{... | collective-permute-start | bytes 4718600 | tf_op jit(solution)/shard_map/ppermute | solution.py:2128
  319.8 1.8 collective-permute-start.1
  321.6 29.6 %shard_map.249 = (bf16[1024,1024]{1,0:T(8,128)(2,1)}, f32[8,128]{1,0:T(8,128)}, f32[8,128]{1,0:T(8,128)}) custom-call(bf16[1024,2048]{1,0:T(8,128)(2,1)} %get-tuple-element.78.hidden_low.hidden_low_hbm, bf16[512,2048]{1,0:T(8,128)(2,1)} %output_weight.1, bf16[1024,512]{1,0:T(8,128)(2,1)} %get-tuple-element.79.queries, ...), custom_call_target="tpu_custom_call" | custom-call | flops 7516192768 | bytes 25165824 | tf_op jit(solution)/shard_map/pallas_call | solution.py:1800
  351.2 0.7 reduce_sum.18
  351.9 0.7 reduce_sum.19
  352.6 0.1 reshape.40
  352.8 0.8 select_maximum_fusion.lines
  353.6 1.3 add.18.gate_ready
  355.0 239.8 %shard_map.250 = (bf16[1024,2048]{1,0:T(8,128)(2,1)}, bf16[1024,2048]{1,0:T(8,128)(2,1)}, f32[256,1536]{1,0:T(8,128)}, f32[256,1536]{1,0:T(8,128)}, f32[264,1024...) custom-call(f32[256,1536]{1,0:T(8,128)} %collective-permute-done.1.g, ...), custom_call_target="tpu_custom_call" | custom-call | flops 25769803776 | bytes 18874368 | tf_op jit(solution)/shard_map/pallas_call | solution.py:1538
  594.8 11.9 %shard_map.251 = (bf16[1024,2048]{1,0:T(8,128)(2,1)}, bf16[1024,2048]{1,0:T(8,128)(2,1)}, f32[256,1536]{1,0:T(8,128)}, f32[256,1536]{1,0:T(8,128)}, f32[512,256]...) custom-call(bf16[1024,2048]{1,0:T(8,128)(2,1)} %get-tuple-element.90, ...), custom_call_target="tpu_custom_call" | custom-call | tf_op jit(solution)/shard_map/pallas_call | solution.py:1868
  (12 shorter events, 0.2 us)
Async XLA Ops:
  2.0 36.2 %collective-permute-start = (f32[192,2048]{1,0:T(8,128)S(1)}, f32[192,2048]{1,0:T(8,128)S(1)}, u32[]{:S(2)}, u32[]{:S(2)}) collective-permute-start(f32[192,2048]{1,0:T(8,128)S(1)} %dynamic-slice_convert_fusion), channel_id=1, source_target_pairs={{0,8},{4,12},{8,0},{12,4},{16,24},{20,28},{24,16},{28,20},{1,9},{5... | collective-permute-start | bytes 4718600 | tf_op jit(solution)/shard_map/ppermute | solution.py:2073
  38.2 1.1 copy-start.1
  311.9 41.7 %collective-permute-start.3 = (f32[256,1536]{1,0:T(8,128)}, f32[256,1536]{1,0:T(8,128)S(1)}, u32[]{:S(2)}, u32[]{:S(2)}) collective-permute-start(f32[256,1536]{1,0:T(8,128)} %get-tuple-element.74), channel_id=1, source_target_pairs={{0,4},{4,0},{8,12},{12,8},{16,20},{20,16},{24,28},{28,24},{1,5},{5... | collective-permute-start | bytes 4718600 | tf_op jit(solution)/shard_map/ppermute | solution.py:2131
  313.5 41.5 %collective-permute-start.2 = (f32[256,1536]{1,0:T(8,128)}, f32[256,1536]{1,0:T(8,128)}, u32[]{:S(2)}, u32[]{:S(2)}) collective-permute-start(f32[256,1536]{1,0:T(8,128)} %get-tuple-element.72), channel_id=1, source_target_pairs={{0,8},{4,12},{24,16},{28,20},{1,9},{5,13},{25,17},{29,21},{2,10},{... | collective-permute-start | bytes 4718600 | tf_op jit(solution)/shard_map/ppermute | solution.py:2128
  319.8 35.2 %collective-permute-start.1 = (f32[256,1536]{1,0:T(8,128)}, f32[256,1536]{1,0:T(8,128)}, u32[]{:S(2)}, u32[]{:S(2)}) collective-permute-start(f32[256,1536]{1,0:T(8,128)} %get-tuple-element.72), channel_id=1, source_target_pairs={{8,16},{12,20},{16,8},{20,12},{9,17},{13,21},{17,9},{21,13},{10,18... | collective-permute-start | bytes 4718600 | tf_op jit(solution)/shard_map/ppermute | solution.py:2128
  321.6 32.0 %copy-start = (f32[256,1536]{1,0:T(8,128)S(1)}, f32[256,1536]{1,0:T(8,128)}, u32[]{:S(2)}) copy-start(f32[256,1536]{1,0:T(8,128)} %get-tuple-element.73) | copy-start | bytes 4718596

commit v2 on v1

--- a/solution.py
+++ b/solution.py
@@ -175,9 +175,9 @@
     low_pair, product_pair, gate_pair, upward_pair, upstream_pair,
     c_landed, n_recv, n_side, u_recv, u_side,
     mixed, output_weight, gate_weight, up_weight, down_weight,
-    x_send, x_recv, back_recv, tok, hid, z_send, low, rows16, tiles, stage, terms,
+    x_send, x_recv, back_recv, tok, hid, z_send, low, rows16, pair16, tiles, stage, terms,
     load_sems, c_sems, x_sems, back_sems, n_sems, n_side_sems, u_sems, u_side_sems,
-    tok_sems, hid_sems, low_sems, wave_sems, tile_sems, stage_sems, term_sems,
+    tok_sems, hid_sems, low_sems, wave_sems, tile_sems, stage_sems, term_sems, join_sems,
 ):
     core, sibling, facing, pair = neighbours()
     depth = gain.shape[1]
@@ -211,7 +211,16 @@
     ]
     x_copies = [remote(x_send.at[k], x_recv.at[k], x_sems, k, facing) for k in range(4)]
     back_copies = [remote(x_send.at[k], back_recv.at[k], back_sems, k, sibling) for k in range(4)]
-    n_copies = [remote(z_send.at[k % 2], n_recv.at[k], n_sems, k, pair) for k in range(4)]
+    part = pl.ds(pl.multiple_of(lax.axis_index("tensor") // 2 * (size // 2), 16), size // 2)
+    n_copies = [
+        remote(z_send.at[k % 2], n_recv.at[k], n_sems, k, pair)
+        if k < 2
+        else remote(z_send.at[k % 2, part], n_recv.at[k, part], n_sems, k, pair)
+        for k in range(4)
+    ]
+    n_joins = [
+        remote(n_recv.at[k, part], n_recv.at[k, part], join_sems, k - 2, facing) for k in (2, 3)
+    ]
     n_sides = [remote(n_recv.at[k], n_side.at[k], n_side_sems, k, sibling) for k in range(4)]
     u_rows = [(0, rest - 2 * size), (rest - 2 * size, size), (rest - size, size)]
     u_buffers = [hid.at[0, pl.ds(0, u_rows[0][1])], z_send.at[0], z_send.at[1]]
@@ -344,8 +353,15 @@
             stage_load(source, index % 2, number).wait()
             loop_rows(number, 16, functools.partial(consume, index % 2))
 
+    def pair_join(k):
+        n_copies[k].wait_recv()
+        n_joins[k - 2].start()
+
     def pair_forward(k):
-        n_copies[k].wait_recv()
+        if k < 2:
+            n_copies[k].wait_recv()
+        else:
+            n_joins[k - 2].wait_recv()
         n_sides[k].start()
 
     def pair_rows(chunks):
@@ -377,14 +393,14 @@
         return copies
 
     def pair_stores(wave):
-        return wave_copies(rows16, upstream_pair, wave_sems.at[1], wave)
+        return wave_copies(pair16, upstream_pair, wave_sems.at[1], wave)
 
     def upstream_wave(wave):
         def consume(which, start, slot, row):
             side = core if which == 0 else 1 - core
             chunk, within = start // size, start % size
             place = pl.multiple_of((2 * chunk + side) * size + within + row.start, 16)
-            rows16[pl.ds(place, row.size), :] = stage[slot, row, :].astype(jnp.bfloat16)
+            pair16[pl.ds(place, row.size), :] = stage[slot, row, :].astype(jnp.bfloat16)
 
         if wave == 0:
             own = [
@@ -457,7 +473,7 @@
                 low[index, rows], up_weight[:, column], preferred_element_type=jnp.float32
             )
             grad = lax.dot_general(
-                rows16[rows],
+                (pair16 if index else rows16)[rows],
                 down_weight[column, :],
                 across_last,
                 preferred_element_type=jnp.float32,
@@ -517,6 +533,7 @@
     for copy in fetches(0):
         copy.start()
     upstream_forward(0)
+    upstream_wave(0)
     attention_chips(0)
     u_copies[0].wait_send()
     upstream_forward(1)
@@ -542,11 +559,12 @@
     normed(3)
     feed(1, 0, 1)
     pair_forward(1)
-    upstream_wave(0)
     pair_rows((0, 1))
+    pair_join(2)
     feed(0, 1)
     for copy in pair_stores(0):
         copy.wait()
+    pair_join(3)
     pair_forward(2)
     upstream_wave(1)
     for copy in low_stores(0, 1):
@@ -563,6 +581,7 @@
         u_sides[k].wait_send()
         if k >= 2:
             n_copies[k].wait_send()
+            n_joins[k - 2].wait_send()
     ends = hidden_stores(3) + term_stores(1) + low_stores(1, 0) + low_stores(1, 1)
     for copy in ends + pair_stores(1) + tile_stores(1, 1):
         copy.wait()
@@ -601,6 +620,7 @@
             vmem((2, size, depth), f32),
             vmem((2, 4 * size, depth), b16),
             vmem((4 * size, depth), b16),
+            vmem((4 * size, depth), b16),
             vmem((3, 4 * size, units), b16),
             vmem((2, size, depth), f32),
             vmem((4 * size, depth), f32),
@@ -615,6 +635,7 @@
             dma((3, 4)),
             dma((2,)),
             dma((4,)),
+            dma((2, 2)),
         ],
         compiler_params=pltpu.CompilerParams(
             collective_id=1, has_side_effects=True, vmem_limit_bytes=63 * 1024 * 1024

time: 617 us -> 612 us (level)
  no operation moved by 1% of the time
where the time goes in v2:
time: 612 us; the launch traced here: 601 us
  Pallas kernels  577 us (94%)
  other arithmetic  9.64 us (2%)
  starting transfers between devices  6.78 us (1%)
    pallas_call x1, Pallas kernels, rear(): pl.pallas_call(functools.partial(rear_kernel, size, turns), out_shape=[sh...  239 us
    pallas_call x1, Pallas kernels, front(): pl.pallas_call(functools.partial(front_kernel, size, first), out_shape=ou...  157 us
    pallas_call x1, Pallas kernels, middle(): pl.pallas_call(functools.partial(middle_kernel, size), out_shape=[shape((...  114 us
    pallas_call x1, Pallas kernels, attention_back(): pl.pallas_call(functools.partial(attention_back_kernel, 256), out_shape=[...  29.6 us
    pallas_call x1, Pallas kernels, attention(): pl.pallas_call(functools.partial(attention_kernel, 256), out_shape=[shape...  25.9 us
  transfers between devices with their start and end apart: 4, of which 1 were waited for; matrix products, arithmetic and copies ran while one was open for 2% of the time, Pallas kernels for 9%

profile of v2, /device:TPU:24, one launch (start us, length us, event | category | flops | bytes accessed | tf_op | source)
XLA Modules:
  0.0 601.3 jit_solution(8987840996842892920)
XLA Ops:
  0.7 1.3 dynamic-slice_convert_fusion
  2.0 0.5 collective-permute-start
  2.5 0.7 convert_element_type.11
  3.2 1.7 copy.28.segment_column
  4.9 0.2 broadcast_multiply_fusion
  5.1 2.7 fusion
  7.8 0.2 slice_negate_fusion
  8.0 1.0 pad_maximum_fusion.1.sine
  9.0 25.9 %shard_map.246 = (bf16[1024,2048]{1,0:T(8,128)(2,1)}, f32[1024,512]{1,0:T(8,128)}, f32[1024,256]{1,0:T(8,128)}, bf16[1024,512]{1,0:T(8,128)(2,1)}, bf16[1024,256...) custom-call(bf16[1024,2048]{1,0:T(8,128)(2,1)} %tokens_hbm.3, ...), custom_call_target="tpu_custom_call" | custom-call | flops 6442450944 | bytes 33554432 | tf_op jit(solution)/shard_map/pallas_call | solution.py:1705
  34.9 3.2 collective-permute-done.upstream_first
  38.2 1.1 copy-done.1
  39.3 156.8 %shard_map.247 = (f32[1024,2048]{1,0:T(8,128)}, f32[1024,2048]{1,0:T(8,128)}, bf16[1024,2048]{1,0:T(8,128)(2,1)}, bf16[1024,1536]{1,0:T(8,128)(2,1)}, bf16[1024,...) custom-call(bf16[1024,512]{1,0:T(8,128)(2,1)} %get-tuple-element.62., ...), custom_call_target="tpu_custom_call" | custom-call | flops 38654705664 | bytes 18874368 | tf_op jit(solution)/shard_map/pallas_call | solution.py:604
  196.2 114.5 %shard_map.248 = (f32[1024,2048]{1,0:T(8,128)}, bf16[1024,2048]{1,0:T(8,128)(2,1)}, f32[1024,2048]{1,0:T(8,128)}, f32[1536,256]{1,0:T(8,128)}, f32[256,1536]{1,0...) custom-call(f32[1024,2048]{1,0:T(8,128)} %get-tuple-element.63.second_hbm, ...), custom_call_target="tpu_custom_call" | custom-call | flops 25769803776 | bytes 18874368 | tf_op jit(solution)/shard_map/pallas_call | solution.py:982
  310.7 1.0 collective-permute-start.3
  311.6 3.4 collective-permute-start.2
  315.1 1.8 collective-permute-start.1
  316.9 29.6 %shard_map.249 = (bf16[1024,1024]{1,0:T(8,128)(2,1)}, f32[8,128]{1,0:T(8,128)}, f32[8,128]{1,0:T(8,128)}) custom-call(bf16[1024,2048]{1,0:T(8,128)(2,1)} %get-tuple-element.78.hidden_low.hidden_low_hbm, bf16[512,2048]{1,0:T(8,128)(2,1)} %output_weight.1, bf16[1024,512]{1,0:T(8,128)(2,1)} %get-tuple-element.79.queries, ...), custom_call_target="tpu_custom_call" | custom-call | flops 7516192768 | bytes 25165824 | tf_op jit(solution)/shard_map/pallas_call | solution.py:1821
  346.5 0.7 reduce_sum.18
  347.2 0.7 reduce_sum.19
  347.9 0.1 reshape.40
  348.2 0.8 select_maximum_fusion.lines
  348.9 1.3 add.18.gate_ready
  350.3 238.6 %shard_map.250 = (bf16[1024,2048]{1,0:T(8,128)(2,1)}, bf16[1024,2048]{1,0:T(8,128)(2,1)}, f32[256,1536]{1,0:T(8,128)}, f32[256,1536]{1,0:T(8,128)}, f32[264,1024...) custom-call(f32[256,1536]{1,0:T(8,128)} %collective-permute-done.1.g, ...), custom_call_target="tpu_custom_call" | custom-call | flops 25769803776 | bytes 18874368 | tf_op jit(solution)/shard_map/pallas_call | solution.py:1559
  588.9 11.9 %shard_map.251 = (bf16[1024,2048]{1,0:T(8,128)(2,1)}, bf16[1024,2048]{1,0:T(8,128)(2,1)}, f32[256,1536]{1,0:T(8,128)}, f32[256,1536]{1,0:T(8,128)}, f32[512,256]...) custom-call(bf16[1024,2048]{1,0:T(8,128)(2,1)} %get-tuple-element.90, ...), custom_call_target="tpu_custom_call" | custom-call | tf_op jit(solution)/shard_map/pallas_call | solution.py:1889
  (12 shorter events, 0.2 us)
Async XLA Ops:
  2.0 36.2 %collective-permute-start = (f32[192,2048]{1,0:T(8,128)S(1)}, f32[192,2048]{1,0:T(8,128)S(1)}, u32[]{:S(2)}, u32[]{:S(2)}) collective-permute-start(f32[192,2048]{1,0:T(8,128)S(1)} %dynamic-slice_convert_fusion), channel_id=1, source_target_pairs={{0,8},{4,12},{8,0},{12,4},{16,24},{20,28},{24,16},{28,20},{1,9},{5... | collective-permute-start | bytes 4718600 | tf_op jit(solution)/shard_map/ppermute | solution.py:2094
  38.2 1.1 copy-start.1
  310.7 38.3 %collective-permute-start.3 = (f32[256,1536]{1,0:T(8,128)}, f32[256,1536]{1,0:T(8,128)S(1)}, u32[]{:S(2)}, u32[]{:S(2)}) collective-permute-start(f32[256,1536]{1,0:T(8,128)} %get-tuple-element.74), channel_id=1, source_target_pairs={{0,4},{4,0},{8,12},{12,8},{16,20},{20,16},{24,28},{28,24},{1,5},{5... | collective-permute-start | bytes 4718600 | tf_op jit(solution)/shard_map/ppermute | solution.py:2152
  311.6 38.6 %collective-permute-start.2 = (f32[256,1536]{1,0:T(8,128)}, f32[256,1536]{1,0:T(8,128)}, u32[]{:S(2)}, u32[]{:S(2)}) collective-permute-start(f32[256,1536]{1,0:T(8,128)} %get-tuple-element.72), channel_id=1, source_target_pairs={{0,8},{4,12},{24,16},{28,20},{1,9},{5,13},{25,17},{29,21},{2,10},{... | collective-permute-start | bytes 4718600 | tf_op jit(solution)/shard_map/ppermute | solution.py:2149
  315.1 35.2 %collective-permute-start.1 = (f32[256,1536]{1,0:T(8,128)}, f32[256,1536]{1,0:T(8,128)}, u32[]{:S(2)}, u32[]{:S(2)}) collective-permute-start(f32[256,1536]{1,0:T(8,128)} %get-tuple-element.72), channel_id=1, source_target_pairs={{8,16},{12,20},{16,8},{20,12},{9,17},{13,21},{17,9},{21,13},{10,18... | collective-permute-start | bytes 4718600 | tf_op jit(solution)/shard_map/ppermute | solution.py:2149
  316.9 32.0 %copy-start = (f32[256,1536]{1,0:T(8,128)S(1)}, f32[256,1536]{1,0:T(8,128)}, u32[]{:S(2)}) copy-start(f32[256,1536]{1,0:T(8,128)} %get-tuple-element.73) | copy-start | bytes 4718596

commit v3 on v2

--- a/solution.py
+++ b/solution.py
@@ -1094,7 +1094,7 @@
     query_hbm, key_hbm, value_hbm, gate_hbm, up_hbm, gain, feed_gain,
     layer_out, tokens_out, gate_out, up_out, raw_out, head_out, gains_out,
     o_c, o_x, o_back, d_c, d_x, d_back, gate_landed, up_landed,
-    upwards, raw, mixed, head_weights, feed_rows, gains, gain_rows, gains_in, columns,
+    upwards, raw, mixed, head_weights, feed_rows, gains, gain_rows, gains_in, gains_sum, columns,
     up_send, up_kept, raw_send, raw_kept, head_send, head_kept, raw_line, head_line,
     own, give, stage, wide, narrow, result,
     load_sems, column_sems, y_up_sems, y_raw_sems, y_head_sems, gate_sems, up_sems,
@@ -1162,7 +1162,8 @@
     ]
     for copy in column_loads(0) + loads[:2] + column_loads(1) + own_loads + loads[2:]:
         copy.start()
-    greet_grid([sibling, facing, across, inward], inner, outward)
+    opposite = {"tensor": lax.rem(lax.axis_index("tensor") + 3 - 2 * core, 4)}
+    greet_grid([sibling, facing, opposite, across, inward], inner, outward)
     devices = (sibling, facing)
     outs = TensorSum(
         size, own, (o_c, o_x, o_back), stage, (oc_sems, ox_sems, ob_sems), stage_sems, devices
@@ -1521,13 +1522,14 @@
     gain_rows[8:, :] = raw_kept[high - 1, width:, :width]
     gain_copies = [
         remote(gain_rows, gains_in.at[k], gain_sems, k, device)
-        for k, device in enumerate((sibling, facing))
+        for k, device in enumerate((sibling, facing, opposite))
     ]
-    for k in range(2):
-        gain_copies[k].start()
-        gain_copies[k].wait()
-        gain_rows[...] = gain_rows[...] + gains_in[k]
-    gain_store = pltpu.make_async_copy(gain_rows, gains_out, own_sems.at[0])
+    for copy in gain_copies:
+        copy.start()
+    for copy in gain_copies:
+        copy.wait()
+    gains_sum[...] = (gain_rows[...] + gains_in[0]) + (gains_in[1] + gains_in[2])
+    gain_store = pltpu.make_async_copy(gains_sum, gains_out, own_sems.at[0])
     gain_store.start()
     gain_store.wait()
     for k in range(4):
@@ -1579,7 +1581,8 @@
             vmem((2, width, units), b16),
             vmem((width, HD), f32),
             vmem((16, width), f32),
-            vmem((2, 16, width), f32),
+            vmem((3, 16, width), f32),
+            vmem((16, width), f32),
             vmem((2, 2 * rows, width), b16),
             vmem((2, width, units), f32),
             vmem((2, width, units), f32),
@@ -1611,7 +1614,7 @@
             dma((2,)),
             dma((2,)),
             dma((6,)),
-            dma((2, 2)),
+            dma((2, 3)),
         ],
         compiler_params=pltpu.CompilerParams(
             collective_id=3, has_side_effects=True, vmem_limit_bytes=62 * 1024 * 1024
@@ -2092,7 +2095,7 @@
     high = dp // 2
     core = lax.axis_index("tensor") % 2
     upstream_first = lax.ppermute(
-        lax.dynamic_slice_in_dim(cotangent, core * (count // 2), 3 * count // 16, 0).astype(jnp.float32),
+        lax.dynamic_slice_in_dim(cotangent, core * (count // 2), 11 * count // 64, 0).astype(jnp.float32),
         "dp",
         [(i, i ^ 2) for i in range(dp)],
     )

time: 612 us -> 611 us (level)
  no operation moved by 1% of the time
where the time goes in v3:
time: 611 us; the launch traced here: 600 us
  Pallas kernels  580 us (95%)
  other arithmetic  9.6 us (2%)
  starting transfers between devices  6.69 us (1%)
    pallas_call x1, Pallas kernels, rear(): pl.pallas_call(functools.partial(rear_kernel, size, turns), out_shape=[sh...  238 us
    pallas_call x1, Pallas kernels, front(): pl.pallas_call(functools.partial(front_kernel, size, first), out_shape=ou...  160 us
    pallas_call x1, Pallas kernels, middle(): pl.pallas_call(functools.partial(middle_kernel, size), out_shape=[shape((...  115 us
    pallas_call x1, Pallas kernels, attention_back(): pl.pallas_call(functools.partial(attention_back_kernel, 256), out_shape=[...  29.6 us
    pallas_call x1, Pallas kernels, attention(): pl.pallas_call(functools.partial(attention_kernel, 256), out_shape=[shape...  25.9 us
  transfers between devices with their start and end apart: 4, of which 1 were waited for; matrix products, arithmetic and copies ran while one was open for 2% of the time, Pallas kernels for 9%

profile of v3, /device:TPU:24, one launch (start us, length us, event | category | flops | bytes accessed | tf_op | source)
XLA Modules:
  0.0 600.4 jit_solution(16074819885583318334)
XLA Ops:
  0.7 1.3 dynamic-slice_convert_fusion
  1.9 0.5 collective-permute-start
  2.4 0.7 convert_element_type.11
  3.1 1.7 copy.28.segment_column
  4.8 0.2 broadcast_multiply_fusion
  5.0 2.7 fusion
  7.8 0.2 slice_negate_fusion
  8.0 1.0 pad_maximum_fusion.1.sine
  9.0 25.9 %shard_map.246 = (bf16[1024,2048]{1,0:T(8,128)(2,1)}, f32[1024,512]{1,0:T(8,128)}, f32[1024,256]{1,0:T(8,128)}, bf16[1024,512]{1,0:T(8,128)(2,1)}, bf16[1024,256...) custom-call(bf16[1024,2048]{1,0:T(8,128)(2,1)} %tokens_hbm.3, ...), custom_call_target="tpu_custom_call" | custom-call | flops 6442450944 | bytes 33554432 | tf_op jit(solution)/shard_map/pallas_call | solution.py:1708
  34.9 0.4 collective-permute-done.upstream_first
  35.3 1.1 copy-done.1
  36.4 159.7 %shard_map.247 = (f32[1024,2048]{1,0:T(8,128)}, f32[1024,2048]{1,0:T(8,128)}, bf16[1024,2048]{1,0:T(8,128)(2,1)}, bf16[1024,1536]{1,0:T(8,128)(2,1)}, bf16[1024,...) custom-call(bf16[1024,512]{1,0:T(8,128)(2,1)} %get-tuple-element.62., ...), custom_call_target="tpu_custom_call" | custom-call | flops 38654705664 | bytes 18874368 | tf_op jit(solution)/shard_map/pallas_call | solution.py:604
  196.1 114.6 %shard_map.248 = (f32[1024,2048]{1,0:T(8,128)}, bf16[1024,2048]{1,0:T(8,128)(2,1)}, f32[1024,2048]{1,0:T(8,128)}, f32[1536,256]{1,0:T(8,128)}, f32[256,1536]{1,0...) custom-call(f32[1024,2048]{1,0:T(8,128)} %get-tuple-element.63.second_hbm, ...), custom_call_target="tpu_custom_call" | custom-call | flops 25769803776 | bytes 18874368 | tf_op jit(solution)/shard_map/pallas_call | solution.py:982
  310.7 1.5 collective-permute-start.3
  312.1 2.9 collective-permute-start.2
  315.0 1.8 collective-permute-start.1
  316.9 29.6 %shard_map.249 = (bf16[1024,1024]{1,0:T(8,128)(2,1)}, f32[8,128]{1,0:T(8,128)}, f32[8,128]{1,0:T(8,128)}) custom-call(bf16[1024,2048]{1,0:T(8,128)(2,1)} %get-tuple-element.78.hidden_low.hidden_low_hbm, bf16[512,2048]{1,0:T(8,128)(2,1)} %output_weight.1, bf16[1024,512]{1,0:T(8,128)(2,1)} %get-tuple-element.79.queries, ...), custom_call_target="tpu_custom_call" | custom-call | flops 7516192768 | bytes 25165824 | tf_op jit(solution)/shard_map/pallas_call | solution.py:1824
  346.4 0.7 reduce_sum.18
  347.1 0.7 reduce_sum.19
  347.8 0.1 reshape.40
  348.1 0.8 select_maximum_fusion.lines
  348.9 1.3 add.18.gate_ready
  350.2 237.8 %shard_map.250 = (bf16[1024,2048]{1,0:T(8,128)(2,1)}, bf16[1024,2048]{1,0:T(8,128)(2,1)}, f32[256,1536]{1,0:T(8,128)}, f32[256,1536]{1,0:T(8,128)}, f32[264,1024...) custom-call(f32[256,1536]{1,0:T(8,128)} %collective-permute-done.1.g, ...), custom_call_target="tpu_custom_call" | custom-call | flops 25769803776 | bytes 18874368 | tf_op jit(solution)/shard_map/pallas_call | solution.py:1561
  588.1 11.9 %shard_map.251 = (bf16[1024,2048]{1,0:T(8,128)(2,1)}, bf16[1024,2048]{1,0:T(8,128)(2,1)}, f32[256,1536]{1,0:T(8,128)}, f32[256,1536]{1,0:T(8,128)}, f32[512,256]...) custom-call(bf16[1024,2048]{1,0:T(8,128)(2,1)} %get-tuple-element.90, ...), custom_call_target="tpu_custom_call" | custom-call | tf_op jit(solution)/shard_map/pallas_call | solution.py:1892
  (12 shorter events, 0.2 us)
Async XLA Ops:
  1.9 33.4 %collective-permute-start = (f32[176,2048]{1,0:T(8,128)S(1)}, f32[176,2048]{1,0:T(8,128)S(1)}, u32[]{:S(2)}, u32[]{:S(2)}) collective-permute-start(f32[176,2048]{1,0:T(8,128)S(1)} %dynamic-slice_convert_fusion), channel_id=1, source_target_pairs={{0,8},{4,12},{8,0},{12,4},{16,24},{20,28},{24,16},{28,20},{1,9},{5... | collective-permute-start | bytes 4325384 | tf_op jit(solution)/shard_map/ppermute | solution.py:2097
  35.3 1.1 copy-start.1
  310.7 38.2 %collective-permute-start.3 = (f32[256,1536]{1,0:T(8,128)}, f32[256,1536]{1,0:T(8,128)S(1)}, u32[]{:S(2)}, u32[]{:S(2)}) collective-permute-start(f32[256,1536]{1,0:T(8,128)} %get-tuple-element.74), channel_id=1, source_target_pairs={{0,4},{4,0},{8,12},{12,8},{16,20},{20,16},{24,28},{28,24},{1,5},{5... | collective-permute-start | bytes 4718600 | tf_op jit(solution)/shard_map/ppermute | solution.py:2155
  312.1 38.1 %collective-permute-start.2 = (f32[256,1536]{1,0:T(8,128)}, f32[256,1536]{1,0:T(8,128)}, u32[]{:S(2)}, u32[]{:S(2)}) collective-permute-start(f32[256,1536]{1,0:T(8,128)} %get-tuple-element.72), channel_id=1, source_target_pairs={{0,8},{4,12},{24,16},{28,20},{1,9},{5,13},{25,17},{29,21},{2,10},{... | collective-permute-start | bytes 4718600 | tf_op jit(solution)/shard_map/ppermute | solution.py:2152
  315.0 35.2 %collective-permute-start.1 = (f32[256,1536]{1,0:T(8,128)}, f32[256,1536]{1,0:T(8,128)}, u32[]{:S(2)}, u32[]{:S(2)}) collective-permute-start(f32[256,1536]{1,0:T(8,128)} %get-tuple-element.72), channel_id=1, source_target_pairs={{8,16},{12,20},{16,8},{20,12},{9,17},{13,21},{17,9},{21,13},{10,18... | collective-permute-start | bytes 4718600 | tf_op jit(solution)/shard_map/ppermute | solution.py:2152
  316.9 32.0 %copy-start = (f32[256,1536]{1,0:T(8,128)S(1)}, f32[256,1536]{1,0:T(8,128)}, u32[]{:S(2)}) copy-start(f32[256,1536]{1,0:T(8,128)} %get-tuple-element.73) | copy-start | bytes 4718596
